TPU v7x, 256 devices: a whole 4x4x8 slice. The times are simulated.
256 devices in a mesh: dom: 256 (over x, y, z, core).
Axes of the slice: x: 4, y: 4, z: 8, core: 2. Of those that a mesh axis runs over, the one named last changes fastest.
Arguments:
- x_block: float32 [8, 393216], P(None, 'dom'), may hold values from -18 to 18
- p_block: float32 [8, 393216], P(None, 'dom'), may hold values from -18 to 18
- stiff_elem: float32 [20, 20, 65536], P(None, None, 'dom'), may hold values from -6 to 12.4, as said below
- mass_elem: float32 [20, 20, 65536], P(None, None, 'dom'), may hold values from -0.03 to 0.7, as said below
- node_elem: float32 [10, 10, 65536], P(None, None, 'dom'), may hold values from -1 to 6.1, as said below
- elem_edge: int32 [20, 65536], P(None, 'dom'), may hold values from 0 to 1919, as said below
- elem_node: int32 [10, 65536], P(None, 'dom'), may hold values from 0 to 575, as said below
- send_edge: int32 [6, 16384], P(None, 'dom'), may hold values from 0 to 1535, as said below
- send_node: int32 [6, 8192], P(None, 'dom'), may hold values from 0 to 383, as said below
- grad_pairs: int32 [2, 393216], P(None, 'dom'), may hold values from 0 to 575, as said below
Outputs:
- w_block: float32 [8, 393216], P(None, 'dom')
- gram_stiff: float32 [24, 24], replicated
- gram_mass: float32 [24, 24], replicated
Inputs may be any that keep to these rules, and one draw needn't show every extreme that they name: `stiff_elem`: each element's matrix is symmetric and positive definite. `mass_elem`: each element's matrix is symmetric and positive definite. `node_elem`: each element's matrix is symmetric and positive definite. `elem_edge`: the 20 entries of one element are distinct, and every entry of a subdomain's extended edge list is used by some element of that subdomain. `elem_node`: the 10 entries of one element are distinct, and every entry of a subdomain's extended nodal list is used by some element of that subdomain. `send_edge`: the 64 entries of one direction of one subdomain are distinct. `send_node`: the 32 entries of one direction of one subdomain are distinct. `grad_pairs`: the tail and head of one edge unknown differ.
All inputs are finite; a program needn't handle non-finite values.
Results may differ from a plain program's by a relative error of at most 0.0001.
Values sent between devices are 32-bit elements; how exact they have to be, the bound alone decides.
A program may use at most 128 MiB of HBM per device.

v0:
```python
import jax
import jax.numpy as jnp
from jax import lax
from jax.sharding import PartitionSpec as P

CHEB_DEG = 3
NNODE = 384


highest = lax.Precision.HIGHEST
OFFSETS = (1, -1, 4, -4, 16, -16)
interval_low = 0.3
interval_high = 1.7
jacobi_weight = 0.7


def from_behind(shard, axis, by):
    length = lax.axis_size(axis)
    return lax.ppermute(shard, axis, [(i, (i + by) % length) for i in range(length)])


def edge_extend(values, send_edge):
    pieces = [values]
    for direction in range(6):
        outgoing = values[:, send_edge[direction]]
        pieces.append(from_behind(outgoing, "dom", OFFSETS[direction]))
    return jnp.concatenate(pieces, axis=1)


def edge_return(extended, send_edge):
    ghosts = send_edge.shape[1]
    owned = extended.shape[1] - 6 * ghosts
    total = extended[:, :owned]
    for direction in range(6):
        start = owned + direction * ghosts
        back = from_behind(extended[:, start : start + ghosts], "dom", -OFFSETS[direction])
        total = total.at[:, send_edge[direction]].add(back)
    return total


def node_extend(values, send_node):
    pieces = [values]
    for direction in range(6):
        outgoing = values[:, send_node[direction]]
        pieces.append(from_behind(outgoing, "dom", OFFSETS[direction]))
    return jnp.concatenate(pieces, axis=1)


def node_return(extended, send_node):
    ghosts = send_node.shape[1]
    owned = extended.shape[1] - 6 * ghosts
    total = extended[:, :owned]
    for direction in range(6):
        start = owned + direction * ghosts
        back = from_behind(extended[:, start : start + ghosts], "dom", -OFFSETS[direction])
        total = total.at[:, send_node[direction]].add(back)
    return total


def element_terms(matrices, values):
    return jnp.einsum("jke,cke->cje", matrices, values, precision=highest)


def scatter_local(terms, connect, length):
    return jnp.zeros((terms.shape[0], length), jnp.float32).at[:, connect].add(terms)


def inner_rows(left, right):
    return jnp.einsum("cn,dn->cd", left, right, precision=highest)


def arrange(pair_part, row_part, modes):
    mode_mode = pair_part[:, :modes, :modes]
    mode_prev = pair_part[:, :modes, modes:]
    prev_mode = pair_part[:, modes:, :modes]
    prev_prev = pair_part[:, modes:, modes:]
    new_mode = jnp.swapaxes(row_part[:, :, :modes], 1, 2)
    new_prev = jnp.swapaxes(row_part[:, :, 2 * modes :], 1, 2)
    upper = jnp.concatenate([mode_mode, new_mode, mode_prev], axis=2)
    lower = jnp.concatenate([prev_mode, new_prev, prev_prev], axis=2)
    return jnp.concatenate([upper, row_part, lower], axis=1)


def shards(
    x_block,
    p_block,
    stiff_elem,
    mass_elem,
    node_elem,
    elem_edge,
    elem_node,
    send_edge,
    send_node,
    grad_pairs,
):
    modes = x_block.shape[0]
    owned_edges = x_block.shape[1]
    edge_length = owned_edges + 6 * send_edge.shape[1]
    node_length = NNODE + 6 * send_node.shape[1]
    pair = jnp.concatenate([x_block, p_block], axis=0)
    pair_values = edge_extend(pair, send_edge)[:, elem_edge]
    stiff_pair = element_terms(stiff_elem, pair_values)
    mass_pair = element_terms(mass_elem, pair_values)
    edge_diag = edge_return(
        scatter_local(jnp.einsum("jje->je", stiff_elem)[None], elem_edge, edge_length), send_edge
    )[0]
    node_diag = node_return(
        scatter_local(jnp.einsum("jje->je", node_elem)[None], elem_node, node_length), send_node
    )[0]
    images = edge_return(
        scatter_local(jnp.concatenate([stiff_pair, mass_pair], axis=0), elem_edge, edge_length),
        send_edge,
    )
    stiff_x = images[:modes]
    stiff_p = images[modes : 2 * modes]
    mass_x = images[2 * modes : 3 * modes]
    mass_p = images[3 * modes :]
    numerator, denominator = lax.psum(
        (jnp.sum(x_block * stiff_x, axis=1), jnp.sum(x_block * mass_x, axis=1)), "dom"
    )
    quotient = numerator / denominator
    residual = stiff_x - quotient[:, None] * mass_x

    def stiff_image(vectors):
        values = edge_extend(vectors, send_edge)[:, elem_edge]
        return edge_return(
            scatter_local(element_terms(stiff_elem, values), elem_edge, edge_length), send_edge
        )

    center = 0.5 * (interval_high + interval_low)
    spread = 0.5 * (interval_high - interval_low)
    sigma = center / spread
    rho_now = 1.0 / sigma
    step_dir = residual / (center * edge_diag)
    smooth = step_dir
    for turn in range(CHEB_DEG - 1):
        rho_next = 1.0 / (2.0 * sigma - rho_now)
        remain = residual - stiff_image(smooth)
        step_dir = rho_next * rho_now * step_dir + 2.0 * rho_next / spread * remain / edge_diag
        smooth = smooth + step_dir
        rho_now = rho_next
    after = residual - stiff_image(smooth)
    tails = grad_pairs[0]
    heads = grad_pairs[1]
    gathered_res = (
        jnp.zeros((modes, node_length), jnp.float32)
        .at[:, heads]
        .add(after)
        .at[:, tails]
        .add(-after)
    )
    nodal_res = node_return(gathered_res, send_node)
    first = jacobi_weight * nodal_res / node_diag
    first_values = node_extend(first, send_node)[:, elem_node]
    node_image = node_return(
        scatter_local(element_terms(node_elem, first_values), elem_node, node_length), send_node
    )
    second = first + jacobi_weight * (nodal_res - node_image) / node_diag
    second_full = node_extend(second, send_node)
    w_block = smooth + second_full[:, heads] - second_full[:, tails]
    basis = jnp.concatenate([x_block, w_block, p_block], axis=0)
    w_values = edge_extend(w_block, send_edge)[:, elem_edge]
    stiff_wterm = element_terms(stiff_elem, w_values)
    mass_wterm = element_terms(mass_elem, w_values)
    w_images = edge_return(
        scatter_local(jnp.concatenate([stiff_wterm, mass_wterm], axis=0), elem_edge, edge_length),
        send_edge,
    )
    w_rows = jnp.stack([inner_rows(w_images[:modes], basis), inner_rows(w_images[modes:], basis)])
    stiff_part = inner_rows(pair, jnp.concatenate([stiff_x, stiff_p], axis=0))
    mass_part = inner_rows(pair, jnp.concatenate([mass_x, mass_p], axis=0))
    full_gram = lax.psum(arrange(jnp.stack([stiff_part, mass_part]), w_rows, modes), "dom")
    total_edges = owned_edges * lax.axis_size("dom")
    return (w_block, full_gram[0] / total_edges, full_gram[1] / total_edges)


def solution(mesh):
    in_specs = (
        P(None, "dom"),
        P(None, "dom"),
        P(None, None, "dom"),
        P(None, None, "dom"),
        P(None, None, "dom"),
        P(None, "dom"),
        P(None, "dom"),
        P(None, "dom"),
        P(None, "dom"),
        P(None, "dom"),
    )
    out_specs = (P(None, "dom"), P(), P())
    return jax.shard_map(shards, mesh=mesh, in_specs=in_specs, out_specs=out_specs, check_vma=False)
```

profile of v0, /device:TPU:1, one launch (start us, length us, event | category | flops | bytes accessed | tf_op | source)
XLA Modules:
  0.0 1168.1 jit_solution(15326669690173513750)
XLA Ops:
  22.1 27.6 %scatter_custom_fusion.7 = f32[1920]{0:T(1024)S(1)} fusion(s32[5120]{0:T(1024)S(1)} %reshape.805, f32[5120]{0:T(1024)S(1)} %reshape.865, f32[]{:T(128)} %constant.12.clone.1), kind=kCustom, calls=%fused_computation.356 | custom fusion | flops 5120 | bytes 7684 | tf_op jit(solution)/shard_map/scatter-add | solution.py:65
  76.2 18.8 %gather_fusion.6 = f32[5120,16]{1,0:T(8,128)} fusion(f32[16,1920]{0,1:T(8,128)} %constant_dynamic-update-slice_fusion.2, s32[5120]{0:T(1024)S(1)} %broadcast_clamp_fusion), kind=kCustom, calls=%fused_computation.6 | custom fusion | bytes 675840 | tf_op jit(solution)/shard_map/gather | solution.py:101
  108.9 8.9 fusion.4
  125.9 29.0 %scatter_custom_fusion = f32[32,1920]{0,1:T(8,128)} fusion(s32[5120]{0:T(1024)S(1)} %reshape.805, f32[5120,32]{1,0:T(8,128)} %bitcast.336, f32[]{:T(128)} %constant.12.clone.1), kind=kCustom, calls=%fused_computation.162 | custom fusion | flops 163840 | bytes 246272 | tf_op jit(solution)/shard_map/scatter-add | solution.py:65
  160.8 8.8 collective-permute-start.8
  200.7 90.3 %all-reduce = (f32[8]{0:T(128)S(1)}, f32[8]{0:T(128)S(1)}) all-reduce(f32[8]{0:T(128)S(1)} %get-tuple-element.16, f32[8]{0:T(128)S(1)} %get-tuple-element.15), channel_id=1, replica_groups=mesh['dom'=256] {'dom'}, use_global_device_ids=true, to_apply=%region_8.0 | all-reduce | flops 16 | bytes 128 | tf_op jit(solution)/shard_map/psum | solution.py:118
  309.5 7.8 collective-permute-start.21
  325.7 18.8 %gather_fusion.13 = f32[5120,8]{1,0:T(8,128)} fusion(f32[8,1920]{0,1:T(8,128)} %constant_dynamic-update-slice_fusion.9, s32[5120]{0:T(1024)S(1)} %broadcast_clamp_fusion), kind=kCustom, calls=%fused_computation.13 | custom fusion | bytes 348160 | tf_op jit(solution)/shard_map/gather | solution.py:125
  361.0 29.0 %scatter_custom_fusion.14 = f32[8,1920]{0,1:T(8,128)} fusion(s32[5120]{0:T(1024)S(1)} %reshape.805, f32[5120,8]{1,0:T(8,128)} %copy.192, f32[]{:T(128)} %constant.12.clone.1), kind=kCustom, calls=%fused_computation.159 | custom fusion | flops 40960 | bytes 61952 | tf_op jit(solution)/shard_map/scatter-add | solution.py:65
  391.5 8.7 collective-permute-start.24
  407.2 18.2 %scatter_custom_fusion.43 = f32[576]{0:T(1024)S(1)} fusion(s32[2560]{0:T(1024)S(1)} %reshape.1165, f32[2560]{0:T(1024)S(1)} %reshape.1167, f32[]{:T(128)} %constant.12.clone.1), kind=kCustom, calls=%fused_computation.370 | custom fusion | flops 2560 | bytes 2308 | tf_op jit(solution)/shard_map/scatter-add | solution.py:65
  462.3 8.8 collective-permute-start.33
  479.7 18.8 %gather_fusion.20 = f32[5120,8]{1,0:T(8,128)} fusion(f32[8,1920]{0,1:T(8,128)} %constant_dynamic-update-slice_fusion.16, s32[5120]{0:T(1024)S(1)} %broadcast_clamp_fusion), kind=kCustom, calls=%fused_computation.20 | custom fusion | bytes 348160 | tf_op jit(solution)/shard_map/gather | solution.py:125
  513.3 29.0 %scatter_custom_fusion.21 = f32[8,1920]{0,1:T(8,128)} fusion(s32[5120]{0:T(1024)S(1)} %reshape.805, f32[5120,8]{1,0:T(8,128)} %copy.196, f32[]{:T(128)} %constant.12.clone.1), kind=kCustom, calls=%fused_computation.157 | custom fusion | flops 40960 | bytes 61952 | tf_op jit(solution)/shard_map/scatter-add | solution.py:65
  543.2 11.8 %collective-permute-start.36 = (f32[8,64]{0,1:T(8,128)S(1)}, f32[8,64]{0,1:T(8,128)S(1)}, u32[]{:S(2)}, u32[]{:S(2)}) collective-permute-start(f32[8,64]{0,1:T(8,128)S(1)} %get-tuple-element.48), channel_id=1, source_target_pairs={{0,255},{1,0},{2,1},{3,2},{4,3},{5,4},{6,5},{7,6},{8,7},{9,8},{10,... | collective-permute-start | bytes 6152 | tf_op jit(solution)/shard_map/ppermute | solution.py:19
  599.8 9.2 collective-permute-start.45
  617.9 18.8 %gather_fusion.27 = f32[5120,8]{1,0:T(8,128)} fusion(f32[8,1920]{0,1:T(8,128)} %constant_dynamic-update-slice_fusion.23, s32[5120]{0:T(1024)S(1)} %broadcast_clamp_fusion), kind=kCustom, calls=%fused_computation.27 | custom fusion | bytes 348160 | tf_op jit(solution)/shard_map/gather | solution.py:125
  651.5 29.0 %scatter_custom_fusion.28 = f32[8,1920]{0,1:T(8,128)} fusion(s32[5120]{0:T(1024)S(1)} %reshape.805, f32[5120,8]{1,0:T(8,128)} %copy.200, f32[]{:T(128)} %constant.12.clone.1), kind=kCustom, calls=%fused_computation.155 | custom fusion | flops 40960 | bytes 61952 | tf_op jit(solution)/shard_map/scatter-add | solution.py:65
  681.4 11.9 %collective-permute-start.48 = (f32[8,64]{0,1:T(8,128)S(1)}, f32[8,64]{0,1:T(8,128)S(1)}, u32[]{:S(2)}, u32[]{:S(2)}) collective-permute-start(f32[8,64]{0,1:T(8,128)S(1)} %get-tuple-element.42), channel_id=1, source_target_pairs={{0,255},{1,0},{2,1},{3,2},{4,3},{5,4},{6,5},{7,6},{8,7},{9,8},{10,... | collective-permute-start | bytes 6152 | tf_op jit(solution)/shard_map/ppermute | solution.py:19
  713.4 8.7 collective-permute-start.62
  731.2 9.4 scatter_custom_fusion.35
  740.6 9.4 scatter_custom_fusion.36
  760.1 10.8 collective-permute-start.56
  813.1 11.3 collective-permute-start.69
  853.7 14.6 %scatter_custom_fusion.50 = f32[8,576]{0,1:T(8,128)S(1)} fusion(s32[2560]{0:T(1024)S(1)} %reshape.1165, f32[2560,8]{1,0:T(8,128)} %copy.204, f32[]{:T(128)} %constant.12.clone.1), kind=kCustom, calls=%fused_computation.172 | custom fusion | flops 20480 | bytes 18944 | tf_op jit(solution)/shard_map/scatter-add | solution.py:65
  868.3 11.6 collective-permute-start.72
  920.9 7.8 collective-permute-start.81
  973.4 7.8 collective-permute-start.87
  989.8 18.8 %gather_fusion.49 = f32[5120,8]{1,0:T(8,128)} fusion(f32[8,1920]{0,1:T(8,128)} %constant_dynamic-update-slice_fusion.44, s32[5120]{0:T(1024)S(1)} %copy-done.10), kind=kCustom, calls=%fused_computation.49 | custom fusion | bytes 348160 | tf_op jit(solution)/shard_map/gather | solution.py:162
  1027.8 28.6 %scatter_custom_fusion.57 = f32[16,1920]{0,1:T(8,128)S(1)} fusion(s32[5120]{0:T(1024)} %copy-done.16, f32[5120,16]{1,0:T(8,128)} %bitcast.335, f32[]{:T(128)} %constant.12.clone.1), kind=kCustom, calls=%fused_computation.153 | custom fusion | flops 81920 | bytes 123392 | tf_op jit(solution)/shard_map/scatter-add | solution.py:65
  1056.4 8.3 collective-permute-start.90
  1084.7 82.3 %psum.23 = f32[2,24,24]{2,1,0:T(8,128)S(1)} all-reduce(f32[2,24,24]{2,1,0:T(8,128)S(1)} %fusion.101), channel_id=1, replica_groups=mesh['dom'=256] {'dom'}, use_global_device_ids=true, to_apply=%region_70.0 | all-reduce | flops 1152 | bytes 9216 | tf_op jit(solution)/shard_map/psum | solution.py:172
  (532 shorter events, 533.2 us)
Async XLA Ops:
  4.7 53.0 %collective-permute-start = (f32[16,64]{0,1:T(8,128)}, f32[16,64]{0,1:T(8,128)S(1)}, u32[]{:S(2)}, u32[]{:S(2)}) collective-permute-start(f32[16,64]{0,1:T(8,128)} %bitcast.2), channel_id=1, source_target_pairs={{0,1},{1,2},{2,3},{3,4},{4,5},{5,6},{6,7},{7,8},{8,9},{9,10},{10,1... | collective-permute-start | bytes 12296 | tf_op jit(solution)/shard_map/ppermute | solution.py:19
  9.0 54.1 %collective-permute-start.1 = (f32[16,64]{0,1:T(8,128)}, f32[16,64]{0,1:T(8,128)S(1)}, u32[]{:S(2)}, u32[]{:S(2)}) collective-permute-start(f32[16,64]{0,1:T(8,128)} %bitcast.5), channel_id=1, source_target_pairs={{0,255},{1,0},{2,1},{3,2},{4,3},{5,4},{6,5},{7,6},{8,7},{9,8},{10,... | collective-permute-start | bytes 12296 | tf_op jit(solution)/shard_map/ppermute | solution.py:19
  9.8 61.4 %collective-permute-start.2 = (f32[16,64]{0,1:T(8,128)S(1)}, f32[16,64]{0,1:T(8,128)S(1)}, u32[]{:S(2)}, u32[]{:S(2)}) collective-permute-start(f32[16,64]{0,1:T(8,128)S(1)} %bitcast.344), channel_id=1, source_target_pairs={{0,4},{1,5},{2,6},{3,7},{4,8},{5,9},{6,10},{7,11},{8,12},{9,13},{1... | collective-permute-start | bytes 12296 | tf_op jit(solution)/shard_map/ppermute | solution.py:19
  13.2 58.6 %collective-permute-start.3 = (f32[16,64]{0,1:T(8,128)S(1)}, f32[16,64]{0,1:T(8,128)S(1)}, u32[]{:S(2)}, u32[]{:S(2)}) collective-permute-start(f32[16,64]{0,1:T(8,128)S(1)} %bitcast.343), channel_id=1, source_target_pairs={{0,252},{1,253},{2,254},{3,255},{4,0},{5,1},{6,2},{7,3},{8,4},{9,5... | collective-permute-start | bytes 12296 | tf_op jit(solution)/shard_map/ppermute | solution.py:19
  20.7 51.7 %collective-permute-start.4 = (f32[16,64]{0,1:T(8,128)S(1)}, f32[16,64]{0,1:T(8,128)S(1)}, u32[]{:S(2)}, u32[]{:S(2)}) collective-permute-start(f32[16,64]{0,1:T(8,128)S(1)} %bitcast.342), channel_id=1, source_target_pairs={{0,16},{1,17},{2,18},{3,19},{4,20},{5,21},{6,22},{7,23},{8,24},{9,... | collective-permute-start | bytes 12296 | tf_op jit(solution)/shard_map/ppermute | solution.py:19
  63.0 95.0 %collective-permute-start.12 = (f32[1,64]{1,0:T(1,128)}, f32[1,64]{1,0:T(1,128)}, u32[]{:S(2)}, u32[]{:S(2)}) collective-permute-start(f32[1,64]{1,0:T(1,128)} %get-tuple-element.87), channel_id=1, source_target_pairs={{0,255},{1,0},{2,1},{3,2},{4,3},{5,4},{6,5},{7,6},{8,7},{9,8},{10,... | collective-permute-start | bytes 776 | tf_op jit(solution)/shard_map/ppermute | solution.py:19
  71.2 87.3 %collective-permute-start.13 = (f32[1,64]{1,0:T(1,128)}, f32[1,64]{1,0:T(1,128)}, u32[]{:S(2)}, u32[]{:S(2)}) collective-permute-start(f32[1,64]{1,0:T(1,128)} %get-tuple-element.86), channel_id=1, source_target_pairs={{0,1},{1,2},{2,3},{3,4},{4,5},{5,6},{6,7},{7,8},{8,9},{9,10},{10,1... | collective-permute-start | bytes 776 | tf_op jit(solution)/shard_map/ppermute | solution.py:19
  71.8 87.7 %collective-permute-start.14 = (f32[1,64]{1,0:T(1,128)}, f32[1,64]{1,0:T(1,128)}, u32[]{:S(2)}, u32[]{:S(2)}) collective-permute-start(f32[1,64]{1,0:T(1,128)} %get-tuple-element.85), channel_id=1, source_target_pairs={{0,252},{1,253},{2,254},{3,255},{4,0},{5,1},{6,2},{7,3},{8,4},{9,5... | collective-permute-start | bytes 776 | tf_op jit(solution)/shard_map/ppermute | solution.py:19
  72.4 88.3 %collective-permute-start.15 = (f32[1,64]{1,0:T(1,128)}, f32[1,64]{1,0:T(1,128)}, u32[]{:S(2)}, u32[]{:S(2)}) collective-permute-start(f32[1,64]{1,0:T(1,128)} %get-tuple-element.84), channel_id=1, source_target_pairs={{0,4},{1,5},{2,6},{3,7},{4,8},{5,9},{6,10},{7,11},{8,12},{9,13},{1... | collective-permute-start | bytes 776 | tf_op jit(solution)/shard_map/ppermute | solution.py:19
  159.5 24.2 %collective-permute-start.7 = (f32[32,64]{0,1:T(8,128)S(1)}, f32[32,64]{0,1:T(8,128)S(1)}, u32[]{:S(2)}, u32[]{:S(2)}) collective-permute-start(f32[32,64]{0,1:T(8,128)S(1)} %get-tuple-element.59), channel_id=1, source_target_pairs={{0,1},{1,2},{2,3},{3,4},{4,5},{5,6},{6,7},{7,8},{8,9},{9,10},{10,1... | collective-permute-start | bytes 24584 | tf_op jit(solution)/shard_map/ppermute | solution.py:19
  160.8 25.9 %collective-permute-start.8 = (f32[32,64]{0,1:T(8,128)S(1)}, f32[32,64]{0,1:T(8,128)}, u32[]{:S(2)}, u32[]{:S(2)}) collective-permute-start(f32[32,64]{0,1:T(8,128)S(1)} %get-tuple-element.58), channel_id=1, source_target_pairs={{0,252},{1,253},{2,254},{3,255},{4,0},{5,1},{6,2},{7,3},{8,4},{9,5... | collective-permute-start | bytes 24584 | tf_op jit(solution)/shard_map/ppermute | solution.py:19
  169.6 23.3 %collective-permute-start.10 = (f32[32,64]{0,1:T(8,128)S(1)}, f32[32,64]{0,1:T(8,128)}, u32[]{:S(2)}, u32[]{:S(2)}) collective-permute-start(f32[32,64]{0,1:T(8,128)S(1)} %get-tuple-element.56), channel_id=1, source_target_pairs={{0,240},{1,241},{2,242},{3,243},{4,244},{5,245},{6,246},{7,247},{8... | collective-permute-start | bytes 24584 | tf_op jit(solution)/shard_map/ppermute | solution.py:19
  170.1 25.9 %collective-permute-start.11 = (f32[32,64]{0,1:T(8,128)S(1)}, f32[32,64]{0,1:T(8,128)S(1)}, u32[]{:S(2)}, u32[]{:S(2)}) collective-permute-start(f32[32,64]{0,1:T(8,128)S(1)} %get-tuple-element.55), channel_id=1, source_target_pairs={{0,16},{1,17},{2,18},{3,19},{4,20},{5,21},{6,22},{7,23},{8,24},{9,... | collective-permute-start | bytes 24584 | tf_op jit(solution)/shard_map/ppermute | solution.py:19
  295.8 21.5 %collective-permute-start.18 = (f32[8,64]{0,1:T(8,128)S(1)}, f32[8,64]{0,1:T(8,128)S(1)}, u32[]{:S(2)}, u32[]{:S(2)}) collective-permute-start(f32[8,64]{0,1:T(8,128)S(1)} %bitcast.370), channel_id=1, source_target_pairs={{0,1},{1,2},{2,3},{3,4},{4,5},{5,6},{6,7},{7,8},{8,9},{9,10},{10,1... | collective-permute-start | bytes 6152 | tf_op jit(solution)/shard_map/ppermute | solution.py:19
  400.1 30.5 %collective-permute-start.25 = (f32[8,64]{0,1:T(8,128)}, f32[8,64]{0,1:T(8,128)}, u32[]{:S(2)}, u32[]{:S(2)}) collective-permute-start(f32[8,64]{0,1:T(8,128)} %get-tuple-element.53), channel_id=1, source_target_pairs={{0,1},{1,2},{2,3},{3,4},{4,5},{5,6},{6,7},{7,8},{8,9},{9,10},{10,1... | collective-permute-start | bytes 6152 | tf_op jit(solution)/shard_map/ppermute | solution.py:19
  400.1 33.6 %collective-permute-start.26 = (f32[8,64]{0,1:T(8,128)}, f32[8,64]{0,1:T(8,128)}, u32[]{:S(2)}, u32[]{:S(2)}) collective-permute-start(f32[8,64]{0,1:T(8,128)} %get-tuple-element.52), channel_id=1, source_target_pairs={{0,252},{1,253},{2,254},{3,255},{4,0},{5,1},{6,2},{7,3},{8,4},{9,5... | collective-permute-start | bytes 6152 | tf_op jit(solution)/shard_map/ppermute | solution.py:19
  403.1 33.7 %collective-permute-start.27 = (f32[8,64]{0,1:T(8,128)S(1)}, f32[8,64]{0,1:T(8,128)}, u32[]{:S(2)}, u32[]{:S(2)}) collective-permute-start(f32[8,64]{0,1:T(8,128)S(1)} %get-tuple-element.51), channel_id=1, source_target_pairs={{0,4},{1,5},{2,6},{3,7},{4,8},{5,9},{6,10},{7,11},{8,12},{9,13},{1... | collective-permute-start | bytes 6152 | tf_op jit(solution)/shard_map/ppermute | solution.py:19
  403.1 36.8 %collective-permute-start.28 = (f32[8,64]{0,1:T(8,128)S(1)}, f32[8,64]{0,1:T(8,128)}, u32[]{:S(2)}, u32[]{:S(2)}) collective-permute-start(f32[8,64]{0,1:T(8,128)S(1)} %get-tuple-element.50), channel_id=1, source_target_pairs={{0,240},{1,241},{2,242},{3,243},{4,244},{5,245},{6,246},{7,247},{8... | collective-permute-start | bytes 6152 | tf_op jit(solution)/shard_map/ppermute | solution.py:19
  406.5 36.5 %collective-permute-start.29 = (f32[8,64]{0,1:T(8,128)S(1)}, f32[8,64]{0,1:T(8,128)}, u32[]{:S(2)}, u32[]{:S(2)}) collective-permute-start(f32[8,64]{0,1:T(8,128)S(1)} %get-tuple-element.49), channel_id=1, source_target_pairs={{0,16},{1,17},{2,18},{3,19},{4,20},{5,21},{6,22},{7,23},{8,24},{9,... | collective-permute-start | bytes 6152 | tf_op jit(solution)/shard_map/ppermute | solution.py:19
  696.4 28.8 %collective-permute-start.52 = (f32[8,64]{0,1:T(8,128)S(1)}, f32[8,64]{0,1:T(8,128)S(1)}, u32[]{:S(2)}, u32[]{:S(2)}) collective-permute-start(f32[8,64]{0,1:T(8,128)S(1)} %get-tuple-element.38), channel_id=1, source_target_pairs={{0,240},{1,241},{2,242},{3,243},{4,244},{5,245},{6,246},{7,247},{8... | collective-permute-start | bytes 6152 | tf_op jit(solution)/shard_map/ppermute | solution.py:19
  700.2 27.9 %collective-permute-start.53 = (f32[8,64]{0,1:T(8,128)S(1)}, f32[8,64]{0,1:T(8,128)S(1)}, u32[]{:S(2)}, u32[]{:S(2)}) collective-permute-start(f32[8,64]{0,1:T(8,128)S(1)} %get-tuple-element.37), channel_id=1, source_target_pairs={{0,16},{1,17},{2,18},{3,19},{4,20},{5,21},{6,22},{7,23},{8,24},{9,... | collective-permute-start | bytes 6152 | tf_op jit(solution)/shard_map/ppermute | solution.py:19
  705.6 51.0 %collective-permute-start.60 = (f32[1,32]{1,0:T(1,128)}, f32[1,32]{1,0:T(1,128)}, u32[]{:S(2)}, u32[]{:S(2)}) collective-permute-start(f32[1,32]{1,0:T(1,128)} %get-tuple-element.105), channel_id=1, source_target_pairs={{0,255},{1,0},{2,1},{3,2},{4,3},{5,4},{6,5},{7,6},{8,7},{9,8},{10,... | collective-permute-start | bytes 392 | tf_op jit(solution)/shard_map/ppermute | solution.py:19
  710.0 47.6 %collective-permute-start.61 = (f32[1,32]{1,0:T(1,128)}, f32[1,32]{1,0:T(1,128)}, u32[]{:S(2)}, u32[]{:S(2)}) collective-permute-start(f32[1,32]{1,0:T(1,128)} %get-tuple-element.104), channel_id=1, source_target_pairs={{0,1},{1,2},{2,3},{3,4},{4,5},{5,6},{6,7},{7,8},{8,9},{9,10},{10,1... | collective-permute-start | bytes 392 | tf_op jit(solution)/shard_map/ppermute | solution.py:19
  713.4 46.6 %collective-permute-start.62 = (f32[1,32]{1,0:T(1,128)}, f32[1,32]{1,0:T(1,128)}, u32[]{:S(2)}, u32[]{:S(2)}) collective-permute-start(f32[1,32]{1,0:T(1,128)} %get-tuple-element.103), channel_id=1, source_target_pairs={{0,252},{1,253},{2,254},{3,255},{4,0},{5,1},{6,2},{7,3},{8,4},{9,5... | collective-permute-start | bytes 392 | tf_op jit(solution)/shard_map/ppermute | solution.py:19
  725.1 34.9 %collective-permute-start.63 = (f32[1,32]{1,0:T(1,128)}, f32[1,32]{1,0:T(1,128)}, u32[]{:S(2)}, u32[]{:S(2)}) collective-permute-start(f32[1,32]{1,0:T(1,128)} %get-tuple-element.102), channel_id=1, source_target_pairs={{0,4},{1,5},{2,6},{3,7},{4,8},{5,9},{6,10},{7,11},{8,12},{9,13},{1... | collective-permute-start | bytes 392 | tf_op jit(solution)/shard_map/ppermute | solution.py:19
  760.1 21.7 %collective-permute-start.56 = (f32[8,32]{0,1:T(8,128)S(1)}, f32[8,32]{0,1:T(8,128)}, u32[]{:S(2)}, u32[]{:S(2)}) collective-permute-start(f32[8,32]{0,1:T(8,128)S(1)} %get-tuple-element.70), channel_id=1, source_target_pairs={{0,252},{1,253},{2,254},{3,255},{4,0},{5,1},{6,2},{7,3},{8,4},{9,5... | collective-permute-start | bytes 3080 | tf_op jit(solution)/shard_map/ppermute | solution.py:19
  795.7 32.9 %collective-permute-start.66 = (f32[8,32]{0,1:T(8,128)}, f32[8,32]{0,1:T(8,128)S(1)}, u32[]{:S(2)}, u32[]{:S(2)}) collective-permute-start(f32[8,32]{0,1:T(8,128)} %bitcast.112), channel_id=1, source_target_pairs={{0,1},{1,2},{2,3},{3,4},{4,5},{5,6},{6,7},{7,8},{8,9},{9,10},{10,1... | collective-permute-start | bytes 3080 | tf_op jit(solution)/shard_map/ppermute | solution.py:19
  808.7 25.1 %collective-permute-start.67 = (f32[8,32]{0,1:T(8,128)}, f32[8,32]{0,1:T(8,128)}, u32[]{:S(2)}, u32[]{:S(2)}) collective-permute-start(f32[8,32]{0,1:T(8,128)} %bitcast.113), channel_id=1, source_target_pairs={{0,255},{1,0},{2,1},{3,2},{4,3},{5,4},{6,5},{7,6},{8,7},{9,8},{10,... | collective-permute-start | bytes 3080 | tf_op jit(solution)/shard_map/ppermute | solution.py:19
  810.9 23.6 %collective-permute-start.68 = (f32[8,32]{0,1:T(8,128)}, f32[8,32]{0,1:T(8,128)S(1)}, u32[]{:S(2)}, u32[]{:S(2)}) collective-permute-start(f32[8,32]{0,1:T(8,128)} %bitcast.114), channel_id=1, source_target_pairs={{0,4},{1,5},{2,6},{3,7},{4,8},{5,9},{6,10},{7,11},{8,12},{9,13},{1... | collective-permute-start | bytes 3080 | tf_op jit(solution)/shard_map/ppermute | solution.py:19
  813.1 21.4 %collective-permute-start.69 = (f32[8,32]{0,1:T(8,128)}, f32[8,32]{0,1:T(8,128)S(1)}, u32[]{:S(2)}, u32[]{:S(2)}) collective-permute-start(f32[8,32]{0,1:T(8,128)} %bitcast.115), channel_id=1, source_target_pairs={{0,252},{1,253},{2,254},{3,255},{4,0},{5,1},{6,2},{7,3},{8,4},{9,5... | collective-permute-start | bytes 3080 | tf_op jit(solution)/shard_map/ppermute | solution.py:19
  908.0 20.7 %collective-permute-start.78 = (f32[8,32]{0,1:T(8,128)}, f32[8,32]{0,1:T(8,128)}, u32[]{:S(2)}, u32[]{:S(2)}) collective-permute-start(f32[8,32]{0,1:T(8,128)} %bitcast.128), channel_id=1, source_target_pairs={{0,1},{1,2},{2,3},{3,4},{4,5},{5,6},{6,7},{7,8},{8,9},{9,10},{10,1... | collective-permute-start | bytes 3080 | tf_op jit(solution)/shard_map/ppermute | solution.py:19
  947.3 33.9 %collective-permute-start.84 = (f32[8,64]{0,1:T(8,128)S(1)}, f32[8,64]{0,1:T(8,128)S(1)}, u32[]{:S(2)}, u32[]{:S(2)}) collective-permute-start(f32[8,64]{0,1:T(8,128)S(1)} %bitcast.369), channel_id=1, source_target_pairs={{0,1},{1,2},{2,3},{3,4},{4,5},{5,6},{6,7},{7,8},{8,9},{9,10},{10,1... | collective-permute-start | bytes 6152 | tf_op jit(solution)/shard_map/ppermute | solution.py:19
  (121 other events, 5506.2 us)
where the time goes:
time: 1180 us; the launch traced here: 1170 us
  other arithmetic  374 us (32%)
  local copies, waits for them, and re-layouts  290 us (25%)
  starting transfers between devices  266 us (23%)
  blocking collectives  173 us (15%)
  matrix products  61.6 us (5%)
    ppermute x96, starting transfers between devices, from_behind(): lax.ppermute(shard, axis, [(i, (i + by) % length) for i in range(length)])  266 us
    scatter-add x8, other arithmetic, scatter_local(): jnp.zeros((terms.shape[0], length), jnp.float32).at[:, connect].add(terms)  205 us
    psum x1, blocking collectives, shards(): lax.psum((jnp.sum(x_block * stiff_x, axis=1), jnp.sum(x_block * mass_x, a...  90.3 us
    scatter-add x36, other arithmetic, edge_return(): total = total.at[:, send_edge[direction]].add(back)  87.1 us
    psum x1, blocking collectives, shards(): lax.psum(arrange(jnp.stack([stiff_part, mass_part]), w_rows, modes), 'dom')  82.3 us
    gather x6, local copies, waits for them, and re-layouts, stiff_image(): values = edge_extend(vectors, send_edge)[:, elem_edge]  67.8 us
    dot_general x8, matrix products, element_terms(): return jnp.einsum('jke,cke->cje', matrices, values, precision=highest)  56.3 us
    gather x30, local copies, waits for them, and re-layouts, edge_extend(): outgoing = values[:, send_edge[direction]]  54.6 us
  transfers between devices with their start and end apart: 96, of which 3 were waited for; matrix products, arithmetic and copies ran while one was open for 31% of the time, Pallas kernels for 0%

commit v1 on v0

v1 whole, which is shorter than its diff:
```python
import jax
import jax.numpy as jnp
from jax import lax
from jax.experimental import pallas as pl
from jax.experimental.pallas import tpu as pltpu
from jax.sharding import PartitionSpec as P

CHEB_DEG = 3
OFFSETS = (1, 4, 16)
LOW = 16
LANES = 128
EDOF = 20
NDOF = 10
EB = 12
EG = 15
NB = 3
NG = 5
ECOL = EDOF * 256
NCOL = NDOF * 256
GCOL = 2 * 1536
interval_low = 0.3
interval_high = 1.7
jacobi_weight = 0.7

f32 = jnp.float32
bf16 = jnp.bfloat16
MESH = pl.DeviceIdType.MESH

X_PAIR, X_DIAG, X_IMAGE, X_FIRST, X_NDIAG, X_CHEB = 0, 1, 2, 3, 4, 5
X_NODE = X_CHEB + 5
X_W = X_NODE + 4
COUNTS = (2, 1, 2, 2, 1) + (1,) * 10


def take(values, lanes):
    return jnp.take_along_axis(values, lanes, axis=1)


def split(values):
    high = values.astype(bf16).astype(f32)
    return jnp.concatenate([high, values - high], axis=0).astype(bf16)


def spread_row(row):
    return jnp.broadcast_to(row, (8, row.shape[1]))


def cols(start, size=LANES):
    return pl.ds(pl.multiple_of(start, LANES), size)


def kernel(
    devices,
    x_ref,
    p_ref,
    stiff_ref,
    mass_ref,
    nodal_ref,
    elem_edge_ref,
    elem_node_ref,
    send_edge_ref,
    send_node_ref,
    grad_ref,
    w_ref,
    gram_s_ref,
    gram_m_ref,
    xe,
    pe,
    ve,
    ne,
    vx,
    vp,
    vv,
    nv,
    gv,
    er,
    ec,
    nr,
    nc,
    gr,
    gc,
    sr,
    sc,
    tr,
    tc,
    inv_e,
    inv_n,
    oh_e,
    qm_e,
    oh_n,
    qm_n,
    oh_g,
    qm_g,
    st,
    left,
    basis_t,
    image_t,
    tot,
    tot2,
    res,
    recip,
    step,
    nres,
    nrecip,
    nfirst,
    ntot,
    send_bufs,
    recv_bufs,
    ar_send,
    ar_recv,
    send_sems,
    recv_sems,
    ar_send_sems,
    ar_recv_sems,
):
    me = lax.axis_index("dom")
    low, high = lax.rem(me, LOW), lax.div(me, LOW)
    highs = devices // LOW
    around = []
    for offset in OFFSETS:
        around.append(lax.rem(me + offset, devices))
        around.append(lax.rem(me + devices - offset, devices))
    groups = [
        [high * LOW + lax.rem(low + m, LOW) for m in range(1, LOW)],
        [lax.rem(high + m, highs) * LOW + low for m in range(1, highs)],
    ]

    barrier = pltpu.get_barrier_semaphore()
    everyone = around + groups[0] + groups[1]
    for partner in everyone:
        pl.semaphore_signal(barrier, inc=1, device_id=(partner,), device_id_type=MESH)

    lane8 = lax.broadcasted_iota(jnp.int32, (8, LANES), 1)
    row8 = lax.broadcasted_iota(jnp.int32, (8, LANES), 0)
    lane128 = lax.broadcasted_iota(jnp.int32, (LANES, LANES), 1).astype(f32)
    zero8 = jnp.zeros((8, LANES), f32)

    def launch(e, t):
        for side in range(2):
            pltpu.make_async_remote_copy(
                src_ref=send_bufs[e].at[t],
                dst_ref=recv_bufs[e].at[2 * t + side],
                send_sem=send_sems.at[e],
                recv_sem=recv_sems.at[e],
                device_id=(around[2 * t + side],),
                device_id_type=MESH,
            ).start()

    def whole(e):
        return pltpu.make_async_remote_copy(
            src_ref=recv_bufs[e],
            dst_ref=recv_bufs[e],
            send_sem=send_sems.at[e],
            recv_sem=recv_sems.at[e],
            device_id=(around[0],),
            device_id_type=MESH,
        )

    def arrived(e):
        whole(e).wait_recv()

    def edge_tile(e, i, t, back):
        first, second = (2 * t + 1, 2 * t) if back else (2 * t, 2 * t + 1)
        return jnp.where(lane8 < 64, recv_bufs[e][first, i], recv_bufs[e][second, i])

    def node_tile(e, n, back):
        swap = 1 if back else 0
        if n == 1:
            tile = jnp.where(lane8 < 32, recv_bufs[e][4 ^ swap, 0], recv_bufs[e][5 ^ swap, 0])
            return jnp.where(lane8 < 64, tile, 0.0)
        one = jnp.where(lane8 < 32, recv_bufs[e][0 ^ swap, 0], recv_bufs[e][1 ^ swap, 0])
        two = jnp.where(lane8 < 96, recv_bufs[e][2 ^ swap, 0], recv_bufs[e][3 ^ swap, 0])
        return jnp.where(lane8 < 64, one, two)

    def reduce_start(slot, stage, tile):
        mine = (low, high)[stage]
        ar_send[slot] = tile
        ar_recv[slot, mine] = tile
        for partner in groups[stage]:
            pltpu.make_async_remote_copy(
                src_ref=ar_send.at[slot],
                dst_ref=ar_recv.at[slot, mine],
                send_sem=ar_send_sems.at[slot],
                recv_sem=ar_recv_sems.at[slot],
                device_id=(partner,),
                device_id_type=MESH,
            ).start()

    def reduce_whole(slot, stage):
        part = ar_recv.at[slot, pl.ds(0, (LOW, highs)[stage] - 1)]
        return pltpu.make_async_remote_copy(
            src_ref=part,
            dst_ref=part,
            send_sem=ar_send_sems.at[slot],
            recv_sem=ar_recv_sems.at[slot],
            device_id=(around[0],),
            device_id_type=MESH,
        )

    def reduce_finish(slot, stage):
        reduce_whole(slot, stage).wait_recv()
        parts = [ar_recv[slot, i] for i in range((LOW, highs)[stage])]
        while len(parts) > 1:
            parts = [a + b for a, b in zip(parts[::2], parts[1::2])]
        return parts[0]

    def gather(out, lanes, blocks, count, sources, first, last, unroll):
        def body(i, carry):
            r, c = lanes[i], blocks[i]
            for o, s in zip(out, sources):
                value = zero8 if first == 0 else o[i]
                for k in range(first, last):
                    value = jnp.where(c == k, take(s[k], r), value)
                o[i] = value
            return carry

        lax.fori_loop(0, count, body, 0, unroll=unroll)

    def pick(source, lanes, blocks, t, owned):
        value = zero8
        for k in range(owned):
            value = jnp.where(blocks[t] == k, take(source[k], lanes[t]), value)
        return value

    def returned(inverse, tiles, block, per):
        value = None
        for d in range(6):
            where = inverse[block * 6 + d]
            term = jnp.where(where >= LANES, take(tiles[d // per], where & 127), 0.0)
            value = term if value is None else value + term
        return value

    def index_tables(row, lanes, blocks, i):
        lanes[i] = spread_row(row & 127)
        blocks[i] = spread_row(row >> 7)

    def masks(qm, blocks, count, parts):
        def body(i, carry):
            c = blocks[i]
            for q in range(parts):
                one = jnp.where(c == q, 1.0, 0.0)
                qm[pl.ds(16 * q, 16), cols(i * LANES)] = jnp.concatenate([one, one], 0).astype(bf16)
            return carry

        lax.fori_loop(0, count, body, 0, unroll=2)

    def one_hot(column):
        return jnp.where(jnp.broadcast_to(column, (LANES, LANES)) == lane128, 1.0, 0.0).astype(bf16)

    def columns_of(rows):
        count, width = rows.shape
        padded = -count % 8
        if padded:
            rows = jnp.concatenate([rows, jnp.zeros((padded, width), jnp.int32)], axis=0)
        return (rows & 127).astype(f32).T

    def fill(base, qm, first, last, count, source, unroll=2):
        def body(i, carry):
            term = st[pl.ds(source, 16), cols(i * LANES)]
            for q in range(first, last):
                left[pl.ds(base + 16 * (q - first), 16), cols(i * LANES)] = (
                    term * qm[pl.ds(16 * q, 16), cols(i * LANES)]
                )
            return carry

        lax.fori_loop(0, count, body, 0, unroll=unroll)

    def scatter(rows, width, table):
        return jnp.dot(left[0:rows, 0:width], table[...], preferred_element_type=f32)

    def joined(product, q):
        return product[16 * q : 16 * q + 8] + product[16 * q + 8 : 16 * q + 16]

    def apply(matrix, values, size, group, consume):
        def body(jj, carry):
            for h in range(2):
                total = [None] * group
                for k in range(size):
                    value = values[2 * k + h]
                    for u in range(group):
                        row = matrix[jj * group + u, pl.ds(k, 1), pl.ds(LANES * h, LANES)]
                        term = row * value
                        total[u] = term if k == 0 else total[u] + term
                for u in range(group):
                    carry = consume(2 * (jj * group + u) + h, total[u], carry)
            return carry

        return body

    def shared_rows(ref, width, per, tiles):
        rows = []
        for t in range(tiles):
            pieces = [ref[d : d + 1, :] for d in range(t * per, min(6, (t + 1) * per))]
            missing = per - len(pieces)
            if missing:
                pieces.append(jnp.zeros((1, missing * width), jnp.int32))
            rows.append(jnp.concatenate(pieces, axis=1))
        return rows

    edge_rows = shared_rows(send_edge_ref, 64, 2, 3)
    for t in range(3):
        index_tables(edge_rows[t], sr, sc, t)
    for k in range(EB):
        xe[k] = x_ref[:, LANES * k : LANES * (k + 1)]
        pe[k] = p_ref[:, LANES * k : LANES * (k + 1)]
    for t in range(3):
        send_bufs[X_PAIR][t, 0] = pick(xe, sr, sc, t, EB)
        send_bufs[X_PAIR][t, 1] = pick(pe, sr, sc, t, EB)
    pl.semaphore_wait(barrier, len(everyone))
    for t in range(3):
        launch(X_PAIR, t)

    for j in range(EDOF):
        for h in range(2):
            row = elem_edge_ref[j : j + 1, LANES * h : LANES * (h + 1)]
            index_tables(row, er, ec, 2 * j + h)
    edge_columns = columns_of(elem_edge_ref[...])
    for j in range(EDOF):
        for h in range(2):
            oh_e[256 * j + LANES * h : 256 * j + LANES * (h + 1), :] = one_hot(
                edge_columns[LANES * h : LANES * (h + 1), j : j + 1]
            )
    masks(qm_e, ec, 2 * EDOF, EG)

    for j in range(EDOF):
        for h in range(2):
            diagonal = spread_row(stiff_ref[j, j : j + 1, LANES * h : LANES * (h + 1)])
            st[0:16, 256 * j + LANES * h : 256 * j + LANES * (h + 1)] = split(diagonal)
    fill(0, qm_e, 0, EG, 2 * EDOF, 0)
    product = scatter(16 * EG, ECOL, oh_e)
    for t in range(3):
        send_bufs[X_DIAG][t, 0] = joined(product, EB + t)
        launch(X_DIAG, t)
    for k in range(EB):
        recip[k] = joined(product, k)

    gather([vx], er, ec, 2 * EDOF, [xe], 0, EB, 4)

    def inverse_lists(inverse, rows, lanes, blocks, per, owned):
        tiles = len(rows)
        width = LANES * tiles
        shared = jnp.concatenate(rows, axis=0)
        turned = columns_of(shared)
        table = jnp.concatenate([one_hot(turned[:, t : t + 1]) for t in range(tiles)], axis=0)
        parts = []
        for q in range(0, owned + owned % 2):
            line = []
            for t in range(tiles):
                direction = t * per + lane8 // (LANES // per)
                keep = jnp.logical_and(row8 == direction, blocks[t] == q)
                line.append(jnp.where(keep, LANES + lane8, 0).astype(f32))
            parts.append(jnp.concatenate(line, axis=1))
        found = jnp.dot(
            jnp.concatenate(parts, axis=0).astype(bf16), table, preferred_element_type=f32
        ).astype(jnp.int32)
        for q in range(owned):
            for d in range(6):
                inverse[q * 6 + d] = spread_row(found[8 * q + d : 8 * q + d + 1])

    inverse_lists(inv_e, edge_rows, sr, sc, 2, EB)

    arrived(X_PAIR)
    for t in range(3):
        xe[EB + t] = edge_tile(X_PAIR, 0, t, False)
        pe[EB + t] = edge_tile(X_PAIR, 1, t, False)
    gather([vx], er, ec, 2 * EDOF, [xe], EB, EG, 4)

    def keep_terms(base, store, ghost_base, i, total):
        term = split(total)
        place = cols(i * LANES)
        if store is not None:
            image_t[pl.ds(store, 16), place] = term
        if base is not None:
            st[pl.ds(base, 16), place] = term
            for q in range(EB, EG):
                left[pl.ds(ghost_base + 16 * (q - EB), 16), place] = term * qm_e[pl.ds(16 * q, 16), place]

    def x_consume(base, store, ghost_base):
        def consume(i, total, carry):
            keep_terms(base, store, ghost_base, i, total)
            return carry + total * vx[i]

        return consume

    numerator = lax.fori_loop(0, 5, apply(stiff_ref, vx, EDOF, 4, x_consume(0, 0, 0)), zero8)
    denominator = lax.fori_loop(0, 5, apply(mass_ref, vx, EDOF, 4, x_consume(16, 16, 48)), zero8)
    product = scatter(96, ECOL, oh_e)
    for t in range(3):
        send_bufs[X_IMAGE][t, 0] = joined(product, t)
        send_bufs[X_IMAGE][t, 1] = joined(product, 3 + t)
        launch(X_IMAGE, t)
    numerator = jnp.sum(numerator, axis=1, keepdims=True)
    denominator = jnp.sum(denominator, axis=1, keepdims=True)
    reduce_start(0, 0, jnp.where(lane8 == 0, numerator, jnp.where(lane8 == 1, denominator, 0.0)))
    fill(0, qm_e, 0, EB, 2 * EDOF, 0)
    fill(16 * EB, qm_e, 0, EB, 2 * EDOF, 16)
    product = scatter(32 * EB, ECOL, oh_e)
    for k in range(EB):
        tot[k] = joined(product, k)
        tot2[k] = joined(product, EB + k)
    arrived(X_DIAG)
    tiles = [edge_tile(X_DIAG, 0, t, True) for t in range(3)]
    center = 0.5 * (interval_high + interval_low)
    spread = 0.5 * (interval_high - interval_low)
    for k in range(EB):
        recip[k] = 1.0 / (recip[k] + returned(inv_e, tiles, k, 2))
    reduce_start(1, 1, reduce_finish(0, 0))
    arrived(X_IMAGE)
    for i, total in enumerate((tot, tot2)):
        tiles = [edge_tile(X_IMAGE, i, t, True) for t in range(3)]
        for k in range(EB):
            total[k] = total[k] + returned(inv_e, tiles, k, 2)
            pe_scaled = total[k] * recip[k] * (1.0 / center)
            (ve if i == 0 else step)[k] = pe_scaled
    for t in range(3):
        send_bufs[X_FIRST][t, 0] = pick(ve, sr, sc, t, EB)
        send_bufs[X_FIRST][t, 1] = pick(step, sr, sc, t, EB)
        launch(X_FIRST, t)

    node_rows = shared_rows(send_node_ref, 32, 4, 2)
    for t in range(2):
        index_tables(node_rows[t], tr, tc, t)
    for j in range(NDOF):
        for h in range(2):
            row = elem_node_ref[j : j + 1, LANES * h : LANES * (h + 1)]
            index_tables(row, nr, nc, 2 * j + h)
    node_columns = columns_of(elem_node_ref[...])
    for j in range(NDOF):
        for h in range(2):
            oh_n[256 * j + LANES * h : 256 * j + LANES * (h + 1), :] = one_hot(
                node_columns[LANES * h : LANES * (h + 1), j : j + 1]
            )
    masks(qm_n, nc, 2 * NDOF, NG)

    sums = reduce_finish(1, 1)
    quotient = jnp.broadcast_to(sums[:, 0:1] / sums[:, 1:2], (8, LANES))
    for k in range(EB):
        residual = tot[k] - quotient * tot2[k]
        res[k] = residual
        first_step = residual * recip[k] * (1.0 / center)
        step[k] = first_step
        ve[k] = first_step

    def stiff_image(extend, back):
        gather([vv], er, ec, 2 * EDOF, [ve], 0, EB, 4)
        arrived(extend)
        for t in range(3):
            tile = edge_tile(extend, 0, t, False)
            if extend == X_FIRST:
                tile = tile - quotient * edge_tile(extend, 1, t, False)
            ve[EB + t] = tile
        gather([vv], er, ec, 2 * EDOF, [ve], EB, EG, 4)

        def consume(i, total, carry):
            keep_terms(0, None, 0, i, total)
            return carry

        lax.fori_loop(0, 5, apply(stiff_ref, vv, EDOF, 4, consume), 0)
        product = scatter(48, ECOL, oh_e)
        for t in range(3):
            send_bufs[back][t, 0] = joined(product, t)
            launch(back, t)
        fill(0, qm_e, 0, EB, 2 * EDOF, 0)
        product = scatter(16 * EB, ECOL, oh_e)
        for k in range(EB):
            tot[k] = joined(product, k)
        return back

    def image_block(tiles, k):
        return tot[k] + returned(inv_e, tiles, k, 2)

    sigma = center / spread
    rho_now = 1.0 / sigma
    extend = X_FIRST
    for turn in range(CHEB_DEG - 1):
        rho_next = 1.0 / (2.0 * sigma - rho_now)
        back = X_CHEB + 2 * turn
        stiff_image(extend, back)
        if turn == 0:
            for j in range(NDOF):
                for h in range(2):
                    diagonal = spread_row(nodal_ref[j, j : j + 1, LANES * h : LANES * (h + 1)])
                    st[0:16, 256 * j + LANES * h : 256 * j + LANES * (h + 1)] = split(diagonal)
            fill(0, qm_n, 0, NG, 2 * NDOF, 0)
            product = scatter(16 * NG, NCOL, oh_n)
            for t in range(3):
                send_bufs[X_NDIAG][t, 0] = joined(product, NB + t // 2)
                launch(X_NDIAG, t)
            for k in range(NB):
                nrecip[k] = joined(product, k)
            inverse_lists(inv_n, node_rows, tr, tc, 4, NB)
        else:
            for side in range(2):
                for k in range(EB):
                    row = grad_ref[1 - side : 2 - side, LANES * k : LANES * (k + 1)]
                    index_tables(row, gr, gc, side * EB + k)
            grad_columns = columns_of(grad_ref[...])
            for side in range(2):
                for k in range(EB):
                    oh_g[LANES * (side * EB + k) : LANES * (side * EB + k + 1), :] = one_hot(
                        grad_columns[LANES * k : LANES * (k + 1), 1 - side : 2 - side]
                    )
            masks(qm_g, gc, 2 * EB, NG)
        arrived(back)
        tiles = [edge_tile(back, 0, t, True) for t in range(3)]
        for k in range(EB):
            remain = res[k] - image_block(tiles, k)
            new_step = rho_next * rho_now * step[k] + (2.0 * rho_next / spread) * remain * recip[k]
            step[k] = new_step
            ve[k] = ve[k] + new_step
        extend = back + 1
        for t in range(3):
            send_bufs[extend][t, 0] = pick(ve, sr, sc, t, EB)
            launch(extend, t)
        rho_now = rho_next
    back = X_CHEB + 4
    stiff_image(extend, back)
    arrived(X_NDIAG)
    tiles = [node_tile(X_NDIAG, n, True) for n in range(2)]
    for k in range(NB):
        nrecip[k] = 1.0 / (nrecip[k] + returned(inv_n, tiles, k, 4))
    arrived(back)
    tiles = [edge_tile(back, 0, t, True) for t in range(3)]
    for k in range(EB):
        after = split(res[k] - image_block(tiles, k))
        st[0:16, LANES * k : LANES * (k + 1)] = after
        st[0:16, LANES * (EB + k) : LANES * (EB + k + 1)] = -after

    def node_return(e, qm, width, table, blocks):
        fill(0, qm, NB, NG, blocks, 0)
        product = scatter(32, width, table)
        for t in range(3):
            send_bufs[e][t, 0] = joined(product, t // 2)
            launch(e, t)
        fill(0, qm, 0, NB, blocks, 0)
        product = scatter(48, width, table)
        for k in range(NB):
            ntot[k] = joined(product, k)

    def node_sum(e):
        arrived(e)
        tiles = [node_tile(e, n, True) for n in range(2)]
        return [ntot[k] + returned(inv_n, tiles, k, 4) for k in range(NB)]

    def node_send(e):
        picked = [pick(ne, tr, tc, n, NB) for n in range(2)]
        for t in range(3):
            send_bufs[e][t, 0] = picked[t // 2]
            launch(e, t)

    def node_ghosts(e):
        arrived(e)
        for n in range(2):
            ne[NB + n] = node_tile(e, n, False)

    node_return(X_NODE, qm_g, GCOL, oh_g, 2 * EB)

    gather([vp], er, ec, 2 * EDOF, [pe], 0, EG, 4)

    def p_consume(store):
        def consume(i, total, carry):
            keep_terms(None, store, 0, i, total)
            return carry

        return consume

    lax.fori_loop(0, 5, apply(stiff_ref, vp, EDOF, 4, p_consume(32)), 0)

    for k, total in enumerate(node_sum(X_NODE)):
        nres[k] = total
        first = jacobi_weight * total * nrecip[k]
        nfirst[k] = first
        ne[k] = first
    node_send(X_NODE + 1)
    gather([nv], nr, nc, 2 * NDOF, [ne], 0, NB, 4)
    lax.fori_loop(0, 5, apply(mass_ref, vp, EDOF, 4, p_consume(48)), 0)
    node_ghosts(X_NODE + 1)
    gather([nv], nr, nc, 2 * NDOF, [ne], NB, NG, 4)

    def node_consume(i, total, carry):
        st[pl.ds(0, 16), cols(i * LANES)] = split(total)
        return carry

    lax.fori_loop(0, 5, apply(nodal_ref, nv, NDOF, 2, node_consume), 0)
    node_return(X_NODE + 2, qm_n, NCOL, oh_n, 2 * NDOF)

    def keep_basis(values, base):
        def body(i, carry):
            basis_t[pl.ds(base, 16), cols(i * LANES)] = split(values[i])
            return carry

        lax.fori_loop(0, 2 * EDOF, body, 0, unroll=4)

    keep_basis(vx, 0)
    keep_basis(vp, 32)
    for k, total in enumerate(node_sum(X_NODE + 2)):
        ne[k] = nfirst[k] + jacobi_weight * (nres[k] - total) * nrecip[k]
    node_send(X_NODE + 3)
    gather([gv], gr, gc, 2 * EB, [ne], 0, NB, 4)
    node_ghosts(X_NODE + 3)
    gather([gv], gr, gc, 2 * EB, [ne], NB, NG, 4)
    for k in range(EB):
        total = ve[k] + gv[k] - gv[EB + k]
        ve[k] = total
        w_ref[:, LANES * k : LANES * (k + 1)] = total

    for t in range(3):
        send_bufs[X_W][t, 0] = pick(ve, sr, sc, t, EB)
        launch(X_W, t)
    image_t[96:128, :] = jnp.zeros((32, ECOL), bf16)
    gather([vv], er, ec, 2 * EDOF, [ve], 0, EB, 4)
    arrived(X_W)
    for t in range(3):
        ve[EB + t] = edge_tile(X_W, 0, t, False)
    gather([vv], er, ec, 2 * EDOF, [ve], EB, EG, 4)
    lax.fori_loop(0, 5, apply(stiff_ref, vv, EDOF, 4, p_consume(64)), 0)
    lax.fori_loop(0, 5, apply(mass_ref, vv, EDOF, 4, p_consume(80)), 0)
    keep_basis(vv, 16)
    product = lax.dot_general(
        basis_t[...], image_t[...], (((1,), (1,)), ((), ())), preferred_element_type=f32
    )

    def basis_rows(b):
        rows = joined(product, b)
        return rows + pltpu.roll(rows, LANES - 8, 1)

    x_rows, w_rows, p_rows = basis_rows(0), basis_rows(1), basis_rows(2)
    even = lane8 % 16 < 8
    packed = jnp.where(
        lane8 < 96,
        jnp.where(even, w_rows, pltpu.roll(x_rows, 8, 1)),
        jnp.where(even, pltpu.roll(p_rows, 64, 1), pltpu.roll(p_rows, 40, 1)),
    )
    reduce_start(2, 0, packed)
    reduce_start(3, 1, reduce_finish(2, 0))
    full = reduce_finish(3, 1) * (1.0 / (devices * LANES * EB))
    turned = full.T
    for m, out in enumerate((gram_s_ref, gram_m_ref)):

        def piece(at):
            return full[:, at : at + 8]

        xs, ps, ws = 16 * m, 32 + 16 * m, 64 + 16 * m
        upper = jnp.concatenate([piece(xs + 8), piece(ws + 8), piece(ps + 8)], axis=1)
        middle = jnp.concatenate([piece(xs), piece(ws), piece(ps)], axis=1)
        lower = jnp.concatenate(
            [turned[ps + 8 : ps + 16, :], piece(104 + 16 * m), piece(96 + 16 * m)], axis=1
        )
        out[...] = jnp.concatenate([upper, middle, lower], axis=0)

    for e in range(len(COUNTS)):
        whole(e).wait_send()
    for slot in range(4):
        reduce_whole(slot, slot % 2).wait_send()


def solution(mesh):
    devices = mesh.shape["dom"]

    def shards(*arrays):
        def tiles(*lead):
            return pltpu.VMEM((*lead, 8, LANES), f32)

        def integers(count):
            return pltpu.VMEM((count, 8, LANES), jnp.int32)

        def halves(rows, width):
            return pltpu.VMEM((rows, width), bf16)

        scratch = [
            tiles(EG),
            tiles(EG),
            tiles(EG),
            tiles(NG),
            tiles(2 * EDOF),
            tiles(2 * EDOF),
            tiles(2 * EDOF),
            tiles(2 * NDOF),
            tiles(2 * EB),
            integers(2 * EDOF),
            integers(2 * EDOF),
            integers(2 * NDOF),
            integers(2 * NDOF),
            integers(2 * EB),
            integers(2 * EB),
            integers(3),
            integers(3),
            integers(2),
            integers(2),
            integers(6 * EB),
            integers(6 * NB),
            halves(ECOL, LANES),
            halves(16 * EG, ECOL),
            halves(NCOL, LANES),
            halves(16 * NG, NCOL),
            halves(GCOL, LANES),
            halves(16 * NG, GCOL),
            halves(32, ECOL),
            halves(32 * EB, ECOL),
            halves(48, ECOL),
            halves(128, ECOL),
            tiles(EB),
            tiles(EB),
            tiles(EB),
            tiles(EB),
            tiles(EB),
            tiles(NB),
            tiles(NB),
            tiles(NB),
            tiles(NB),
            [tiles(3, count) for count in COUNTS],
            [tiles(6, count) for count in COUNTS],
            tiles(4),
            tiles(4, max(LOW, devices // LOW)),
            pltpu.SemaphoreType.DMA((len(COUNTS),)),
            pltpu.SemaphoreType.DMA((len(COUNTS),)),
            pltpu.SemaphoreType.DMA((4,)),
            pltpu.SemaphoreType.DMA((4,)),
        ]
        vmem = pl.BlockSpec(memory_space=pltpu.VMEM)
        return pl.pallas_call(
            lambda *refs: kernel(devices, *refs),
            out_shape=(
                jax.ShapeDtypeStruct((8, LANES * EB), f32),
                jax.ShapeDtypeStruct((24, 24), f32),
                jax.ShapeDtypeStruct((24, 24), f32),
            ),
            in_specs=[vmem] * 10,
            out_specs=(vmem, vmem, vmem),
            scratch_shapes=scratch,
            compiler_params=pltpu.CompilerParams(
                collective_id=0, has_side_effects=True, vmem_limit_bytes=56 * 1024 * 1024
            ),
        )(*arrays)

    split_last = P(None, "dom")
    matrices = P(None, None, "dom")
    in_specs = (split_last,) * 2 + (matrices,) * 3 + (split_last,) * 5
    out_specs = (split_last, P(), P())
    return jax.shard_map(shards, mesh=mesh, in_specs=in_specs, out_specs=out_specs, check_vma=False)
```

time: 1180 us -> 115 us (0.10)
  other arithmetic: 374 us -> 0 us
  local copies, waits for them, and re-layouts: 290 us -> 2.74 us
  starting transfers between devices: 266 us -> 0 us
  blocking collectives: 173 us -> 0 us
  Pallas kernels: 0 us -> 111 us
  matrix products: 61.6 us -> 0 us
    scatter-add x64 -> x0, other arithmetic: 346 us -> none  [the longest x8 205 us: scatter_local(): jnp.zeros((terms.shape[0], length), jnp.float32).at[:, connect].add(terms)]
    ppermute x96 -> x0, starting transfers between devices: 266 us -> none  [from_behind(): lax.ppermute(shard, axis, [(i, (i + by) % length) for i in range(length)])]
    gather x56 -> x0, local copies, waits for them, and re-layouts: 211 us -> none  [the longest x6 67.8 us: stiff_image(): values = edge_extend(vectors, send_edge)[:, elem_edge]]
    psum x2 -> x0, blocking collectives: 173 us -> none  [the longest x1 90.3 us: shards(): lax.psum((jnp.sum(x_block * stiff_x, axis=1), jnp.sum(x_block * mass_x, a...]
    pallas_call x0 -> x1, Pallas kernels: none -> 111 us  [shards(): pl.pallas_call(lambda *refs: kernel(devices, *refs), out_shape=(jax.Shape...]
    dot_general x12 -> x0, matrix products: 61.6 us -> none  [the longest x8 56.3 us: element_terms(): return jnp.einsum('jke,cke->cje', matrices, values, precision=highest)]
    unnamed x156 -> x7, local copies, waits for them, and re-layouts: 30.7 us -> 2.74 us
    transpose x14 -> x0, local copies, waits for them, and re-layouts: 23.1 us -> none  [the longest x12 23 us: element_terms(): return jnp.einsum('jke,cke->cje', matrices, values, precision=highest)]
  transfers between devices with their start and end apart: 96 -> 0, of which waited for: 3 -> 0; matrix products, arithmetic and copies ran while one was open for 31% -> 0% of each run, Pallas kernels for 0% -> 0%
where the time goes in v1:
time: 115 us
  Pallas kernels  111 us (97%)
  local copies, waits for them, and re-layouts  2.74 us (2%)
    pallas_call x1, Pallas kernels, shards(): pl.pallas_call(lambda *refs: kernel(devices, *refs), out_shape=(jax.Shape...  111 us
    unnamed x7, local copies, waits for them, and re-layouts  2.74 us

profile of v1, /device:TPU:1, one launch (start us, length us, event | category | flops | bytes accessed | tf_op | source)
XLA Modules:
  0.0 114.6 jit_solution(16120517980127335572)
XLA Ops:
  0.6 111.2 %shard_map.121 = (f32[8,1536]{1,0:T(8,128)}, f32[24,24]{1,0:T(8,128)}, f32[24,24]{1,0:T(8,128)}) custom-call(f32[8,1536]{1,0:T(8,128)} %refs_0_.1, f32[8,1536]{1,0:T(8,128)} %refs_1_.1, f32[20,20,256]{2,1,0:T(8,128)} %refs_2_.1, f32[20,20,256]{2,1,0:T(8,128)} %refs_3_.1, f32[10,10,256]{2,1,0:T(8,128)} %refs_4_.1, s32[20,256]{1,0:T(8,128)} %refs_5_.1, ...), custom_call_target="tpu_custom_call" | custom-call | tf_op jit(solution)/shard_map/pallas_call | solution.py:721
  111.8 0.0 copy-start.1
  111.8 1.4 %copy.16 = f32[8,1536]{1,0:T(8,128)} copy(f32[8,1536]{1,0:T(8,128)} %get-tuple-element.6) | data formatting | bytes 98304
  113.3 0.0 copy-done.1
  113.3 0.0 copy-start
  113.3 0.6 copy.17
  113.9 0.1 copy-done
  114.0 0.6 copy.18
Async XLA Ops:
  111.8 1.4 %copy-start.1 = (f32[24,24]{1,0:T(8,128)S(1)}, f32[24,24]{1,0:T(8,128)}, u32[]{:S(2)}) copy-start(f32[24,24]{1,0:T(8,128)} %get-tuple-element.7) | copy-start | bytes 6916
  113.3 0.7 copy-start

commit v2 on v1

--- a/solution.py
+++ b/solution.py
@@ -14,7 +14,7 @@
 EB = 12
 EG = 15
 NB = 3
-NG = 5
+NG = 6
 ECOL = EDOF * 256
 NCOL = NDOF * 256
 GCOL = 2 * 1536
@@ -26,10 +26,11 @@
 bf16 = jnp.bfloat16
 MESH = pl.DeviceIdType.MESH
 
-X_PAIR, X_DIAG, X_IMAGE, X_FIRST, X_NDIAG, X_CHEB = 0, 1, 2, 3, 4, 5
-X_NODE = X_CHEB + 5
-X_W = X_NODE + 4
-COUNTS = (2, 1, 2, 2, 1) + (1,) * 10
+PAIRS = [(a, b) for a in range(6) for b in range(a, 6) if b != a ^ 1]
+X_PAIR, X_LINK, X_RETURN, X_W = 0, 1, 2, 3
+PLAIN = (2, 2, 1, 1)
+M_DIAG, M_IMAGE, M_CHEB, M_NDIAG, M_NODE = 0, 1, 2, 4, 5
+MERGED = (1, 2, 1, 1, 1, 1, 1)
 
 
 def take(values, lanes):
@@ -53,9 +54,9 @@
     devices,
     x_ref,
     p_ref,
-    stiff_ref,
-    mass_ref,
-    nodal_ref,
+    stiff_hbm,
+    mass_hbm,
+    nodal_hbm,
     elem_edge_ref,
     elem_node_ref,
     send_edge_ref,
@@ -64,6 +65,9 @@
     w_ref,
     gram_s_ref,
     gram_m_ref,
+    stiff_ref,
+    mass_ref,
+    nodal_ref,
     xe,
     pe,
     ve,
@@ -85,6 +89,8 @@
     tc,
     inv_e,
     inv_n,
+    link_e,
+    link_n,
     oh_e,
     qm_e,
     oh_n,
@@ -106,13 +112,30 @@
     ntot,
     send_bufs,
     recv_bufs,
+    near_send,
+    near_recv,
+    far_send,
+    far_recv,
     ar_send,
     ar_recv,
+    load_sems,
     send_sems,
     recv_sems,
+    near_send_sems,
+    near_recv_sems,
+    far_send_sems,
+    far_recv_sems,
     ar_send_sems,
     ar_recv_sems,
 ):
+    loads = [
+        pltpu.make_async_copy(source, target, load_sems.at[i])
+        for i, (source, target) in enumerate(
+            ((stiff_hbm, stiff_ref), (mass_hbm, mass_ref), (nodal_hbm, nodal_ref))
+        )
+    ]
+    for load in loads:
+        load.start()
     me = lax.axis_index("dom")
     low, high = lax.rem(me, LOW), lax.div(me, LOW)
     highs = devices // LOW
@@ -120,18 +143,21 @@
     for offset in OFFSETS:
         around.append(lax.rem(me + offset, devices))
         around.append(lax.rem(me + devices - offset, devices))
+    signed = [o * s for o in OFFSETS for s in (1, -1)]
+    beyond = [lax.rem(me + 2 * devices - signed[a] - signed[b], devices) for a, b in PAIRS]
     groups = [
         [high * LOW + lax.rem(low + m, LOW) for m in range(1, LOW)],
         [lax.rem(high + m, highs) * LOW + low for m in range(1, highs)],
     ]
 
     barrier = pltpu.get_barrier_semaphore()
-    everyone = around + groups[0] + groups[1]
+    everyone = around + beyond + groups[0] + groups[1]
     for partner in everyone:
         pl.semaphore_signal(barrier, inc=1, device_id=(partner,), device_id_type=MESH)
 
     lane8 = lax.broadcasted_iota(jnp.int32, (8, LANES), 1)
     row8 = lax.broadcasted_iota(jnp.int32, (8, LANES), 0)
+    first_half = lane8 < 64
     lane128 = lax.broadcasted_iota(jnp.int32, (LANES, LANES), 1).astype(f32)
     zero8 = jnp.zeros((8, LANES), f32)
 
@@ -161,16 +187,98 @@
 
     def edge_tile(e, i, t, back):
         first, second = (2 * t + 1, 2 * t) if back else (2 * t, 2 * t + 1)
-        return jnp.where(lane8 < 64, recv_bufs[e][first, i], recv_bufs[e][second, i])
-
-    def node_tile(e, n, back):
-        swap = 1 if back else 0
-        if n == 1:
-            tile = jnp.where(lane8 < 32, recv_bufs[e][4 ^ swap, 0], recv_bufs[e][5 ^ swap, 0])
-            return jnp.where(lane8 < 64, tile, 0.0)
-        one = jnp.where(lane8 < 32, recv_bufs[e][0 ^ swap, 0], recv_bufs[e][1 ^ swap, 0])
-        two = jnp.where(lane8 < 96, recv_bufs[e][2 ^ swap, 0], recv_bufs[e][3 ^ swap, 0])
-        return jnp.where(lane8 < 64, one, two)
+        return jnp.where(first_half, recv_bufs[e][first, i], recv_bufs[e][second, i])
+
+    def far_start(e, ghosts):
+        for i, tiles in enumerate(ghosts):
+            turned = [pltpu.roll(tile, 64, 1) for tile in tiles]
+            for n, (a, b) in enumerate(PAIRS):
+                front = (turned if a % 2 else tiles)[a // 2]
+                rear = (tiles if b % 2 else turned)[b // 2]
+                far_send[e][n, i] = front if a == b else jnp.where(first_half, front, rear)
+        for n in range(len(PAIRS)):
+            pltpu.make_async_remote_copy(
+                src_ref=far_send[e].at[n],
+                dst_ref=far_recv[e].at[n],
+                send_sem=far_send_sems.at[e],
+                recv_sem=far_recv_sems.at[e],
+                device_id=(beyond[n],),
+                device_id_type=MESH,
+            ).start()
+
+    def near_start(e, owned, ghosts):
+        for t in range(3):
+            for i in range(len(owned)):
+                near_send[e][2 * t, i] = jnp.where(first_half, owned[i][t], ghosts[i][t])
+                near_send[e][2 * t + 1, i] = jnp.where(first_half, ghosts[i][t], owned[i][t])
+            for side in range(2):
+                pltpu.make_async_remote_copy(
+                    src_ref=near_send[e].at[2 * t + side],
+                    dst_ref=near_recv[e].at[2 * t + side],
+                    send_sem=near_send_sems.at[e],
+                    recv_sem=near_recv_sems.at[e],
+                    device_id=(around[2 * t + side],),
+                    device_id_type=MESH,
+                ).start()
+
+    def near_whole(e):
+        return pltpu.make_async_remote_copy(
+            src_ref=near_recv[e],
+            dst_ref=near_recv[e],
+            send_sem=near_send_sems.at[e],
+            recv_sem=near_recv_sems.at[e],
+            device_id=(around[0],),
+            device_id_type=MESH,
+        )
+
+    def far_whole(e):
+        return pltpu.make_async_remote_copy(
+            src_ref=far_recv[e],
+            dst_ref=far_recv[e],
+            send_sem=far_send_sems.at[e],
+            recv_sem=far_recv_sems.at[e],
+            device_id=(around[0],),
+            device_id_type=MESH,
+        )
+
+    def slot_of(held, other):
+        pair = (min(held, other), max(held, other))
+        return PAIRS.index(pair), (0 if held <= other else 1)
+
+    def make_links(links, i):
+        for t in range(3):
+            places = edge_tile(X_LINK, i, t, False).astype(jnp.int32)
+            for d in range(6):
+                place = spread_row(places[d : d + 1])
+                lower = None if d == 2 * t else slot_of(d, 2 * t + 1)[1]
+                upper = None if d == 2 * t + 1 else slot_of(d, 2 * t)[1]
+                low_at = jnp.zeros_like(place) if lower is None else LANES + 64 * lower + (place & 63)
+                up_at = jnp.zeros_like(place) if upper is None else LANES + 64 * upper + (place & 63)
+                links[t * 6 + d] = jnp.where(place >= LANES, jnp.where(first_half, low_at, up_at), 0)
+
+    def finish_merge(e, totals, links, inverse, owned):
+        near_whole(e).wait_recv()
+        for i, total in enumerate(totals):
+            back = [jnp.where(first_half, near_recv[e][2 * t + 1, i], near_recv[e][2 * t, i]) for t in range(3)]
+            for k in range(owned):
+                total[k] = total[k] + returned(inverse, back, k)
+        far_whole(e).wait_recv()
+        for i, total in enumerate(totals):
+            for t in range(3):
+                value = total[owned + t] + jnp.where(
+                    first_half, near_recv[e][2 * t, i], near_recv[e][2 * t + 1, i]
+                )
+                for d in range(6):
+                    at = links[t * 6 + d]
+                    sources = []
+                    if d != 2 * t:
+                        sources.append(far_recv[e][slot_of(d, 2 * t + 1)[0], i])
+                    if d != 2 * t + 1:
+                        sources.append(far_recv[e][slot_of(d, 2 * t)[0], i])
+                    found = [take(source, at & 127) for source in sources]
+                    term = found[0] if len(found) == 1 else jnp.where(first_half, found[0], found[1])
+                    value = value + jnp.where(at >= LANES, term, 0.0)
+                total[owned + t] = value
 
     def reduce_start(slot, stage, tile):
         mine = (low, high)[stage]
@@ -222,11 +330,11 @@
             value = jnp.where(blocks[t] == k, take(source[k], lanes[t]), value)
         return value
 
-    def returned(inverse, tiles, block, per):
+    def returned(inverse, tiles, block):
         value = None
         for d in range(6):
             where = inverse[block * 6 + d]
-            term = jnp.where(where >= LANES, take(tiles[d // per], where & 127), 0.0)
+            term = jnp.where(where >= LANES, take(tiles[d // 2], where & 127), 0.0)
             value = term if value is None else value + term
         return value
 
@@ -287,17 +395,18 @@
 
         return body
 
-    def shared_rows(ref, width, per, tiles):
+    def shared_rows(ref, width):
         rows = []
-        for t in range(tiles):
-            pieces = [ref[d : d + 1, :] for d in range(t * per, min(6, (t + 1) * per))]
-            missing = per - len(pieces)
-            if missing:
-                pieces.append(jnp.zeros((1, missing * width), jnp.int32))
+        for t in range(3):
+            pieces = []
+            for d in (2 * t, 2 * t + 1):
+                pieces.append(ref[d : d + 1, :])
+                if width < 64:
+                    pieces.append(jnp.full((1, 64 - width), -LANES, jnp.int32))
             rows.append(jnp.concatenate(pieces, axis=1))
         return rows
 
-    edge_rows = shared_rows(send_edge_ref, 64, 2, 3)
+    edge_rows = shared_rows(send_edge_ref, 64)
     for t in range(3):
         index_tables(edge_rows[t], sr, sc, t)
     for k in range(EB):
@@ -322,42 +431,54 @@
             )
     masks(qm_e, ec, 2 * EDOF, EG)
 
+    loads[0].wait()
     for j in range(EDOF):
         for h in range(2):
             diagonal = spread_row(stiff_ref[j, j : j + 1, LANES * h : LANES * (h + 1)])
             st[0:16, 256 * j + LANES * h : 256 * j + LANES * (h + 1)] = split(diagonal)
     fill(0, qm_e, 0, EG, 2 * EDOF, 0)
     product = scatter(16 * EG, ECOL, oh_e)
-    for t in range(3):
-        send_bufs[X_DIAG][t, 0] = joined(product, EB + t)
-        launch(X_DIAG, t)
-    for k in range(EB):
+    for k in range(EG):
         recip[k] = joined(product, k)
 
+    def merge_start(e, totals, lanes, blocks, owned):
+        ghosts = [[total[owned + t] for t in range(3)] for total in totals]
+        far_start(e, ghosts)
+        shares = [[pick(total, lanes, blocks, t, owned) for t in range(3)] for total in totals]
+        near_start(e, shares, ghosts)
+
+    merge_start(M_DIAG, [recip], sr, sc, EB)
+
     gather([vx], er, ec, 2 * EDOF, [xe], 0, EB, 4)
 
-    def inverse_lists(inverse, rows, lanes, blocks, per, owned):
-        tiles = len(rows)
-        width = LANES * tiles
-        shared = jnp.concatenate(rows, axis=0)
-        turned = columns_of(shared)
-        table = jnp.concatenate([one_hot(turned[:, t : t + 1]) for t in range(tiles)], axis=0)
+    def inverse_lists(inverse, rows, lanes, blocks, owned, i):
+        turned = columns_of(jnp.concatenate(rows, axis=0))
+        table = jnp.concatenate([one_hot(turned[:, t : t + 1]) for t in range(3)], axis=0)
         parts = []
         for q in range(0, owned + owned % 2):
             line = []
-            for t in range(tiles):
-                direction = t * per + lane8 // (LANES // per)
-                keep = jnp.logical_and(row8 == direction, blocks[t] == q)
+            for t in range(3):
+                keep = jnp.logical_and(row8 == 2 * t + (lane8 >> 6), blocks[t] == q)
                 line.append(jnp.where(keep, LANES + lane8, 0).astype(f32))
             parts.append(jnp.concatenate(line, axis=1))
         found = jnp.dot(
             jnp.concatenate(parts, axis=0).astype(bf16), table, preferred_element_type=f32
-        ).astype(jnp.int32)
+        )
+        places = [found[8 * q : 8 * q + 8] for q in range(owned)]
+        for t in range(3):
+            send_bufs[X_LINK][t, i] = pick(places, lanes, blocks, t, owned)
         for q in range(owned):
+            place = places[q].astype(jnp.int32)
             for d in range(6):
-                inverse[q * 6 + d] = spread_row(found[8 * q + d : 8 * q + d + 1])
-
-    inverse_lists(inv_e, edge_rows, sr, sc, 2, EB)
+                inverse[q * 6 + d] = spread_row(place[d : d + 1])
+
+    inverse_lists(inv_e, edge_rows, sr, sc, EB, 0)
+    node_rows = shared_rows(send_node_ref, 32)
+    for t in range(3):
+        index_tables(node_rows[t], tr, tc, t)
+    inverse_lists(inv_n, node_rows, tr, tc, NB, 1)
+    for t in range(3):
+        launch(X_LINK, t)
 
     arrived(X_PAIR)
     for t in range(3):
@@ -382,49 +503,48 @@
 
         return consume
 
+    loads[1].wait()
     numerator = lax.fori_loop(0, 5, apply(stiff_ref, vx, EDOF, 4, x_consume(0, 0, 0)), zero8)
     denominator = lax.fori_loop(0, 5, apply(mass_ref, vx, EDOF, 4, x_consume(16, 16, 48)), zero8)
-    product = scatter(96, ECOL, oh_e)
-    for t in range(3):
-        send_bufs[X_IMAGE][t, 0] = joined(product, t)
-        send_bufs[X_IMAGE][t, 1] = joined(product, 3 + t)
-        launch(X_IMAGE, t)
     numerator = jnp.sum(numerator, axis=1, keepdims=True)
     denominator = jnp.sum(denominator, axis=1, keepdims=True)
     reduce_start(0, 0, jnp.where(lane8 == 0, numerator, jnp.where(lane8 == 1, denominator, 0.0)))
+    product = scatter(96, ECOL, oh_e)
+    ghosts = [[joined(product, 3 * i + t) for t in range(3)] for i in range(2)]
+    far_start(M_IMAGE, ghosts)
+    for t in range(3):
+        tot[EB + t] = ghosts[0][t]
+        tot2[EB + t] = ghosts[1][t]
     fill(0, qm_e, 0, EB, 2 * EDOF, 0)
     fill(16 * EB, qm_e, 0, EB, 2 * EDOF, 16)
     product = scatter(32 * EB, ECOL, oh_e)
     for k in range(EB):
         tot[k] = joined(product, k)
         tot2[k] = joined(product, EB + k)
-    arrived(X_DIAG)
-    tiles = [edge_tile(X_DIAG, 0, t, True) for t in range(3)]
+    near_start(
+        M_IMAGE,
+        [[pick(total, sr, sc, t, EB) for t in range(3)] for total in (tot, tot2)],
+        [[total[EB + t] for t in range(3)] for total in (tot, tot2)],
+    )
     center = 0.5 * (interval_high + interval_low)
     spread = 0.5 * (interval_high - interval_low)
-    for k in range(EB):
-        recip[k] = 1.0 / (recip[k] + returned(inv_e, tiles, k, 2))
+    arrived(X_LINK)
+    make_links(link_e, 0)
+    make_links(link_n, 1)
     reduce_start(1, 1, reduce_finish(0, 0))
-    arrived(X_IMAGE)
-    for i, total in enumerate((tot, tot2)):
-        tiles = [edge_tile(X_IMAGE, i, t, True) for t in range(3)]
-        for k in range(EB):
-            total[k] = total[k] + returned(inv_e, tiles, k, 2)
-            pe_scaled = total[k] * recip[k] * (1.0 / center)
-            (ve if i == 0 else step)[k] = pe_scaled
-    for t in range(3):
-        send_bufs[X_FIRST][t, 0] = pick(ve, sr, sc, t, EB)
-        send_bufs[X_FIRST][t, 1] = pick(step, sr, sc, t, EB)
-        launch(X_FIRST, t)
-
-    node_rows = shared_rows(send_node_ref, 32, 4, 2)
-    for t in range(2):
-        index_tables(node_rows[t], tr, tc, t)
+    finish_merge(M_DIAG, [recip], link_e, inv_e, EB)
+    for k in range(EG):
+        recip[k] = 1.0 / recip[k]
+
+    def padded(index):
+        ghost = index - LANES * NB
+        return jnp.where(ghost < 0, index, LANES * NB + ((ghost >> 5) << 6) + (ghost & 31))
+
     for j in range(NDOF):
         for h in range(2):
-            row = elem_node_ref[j : j + 1, LANES * h : LANES * (h + 1)]
+            row = padded(elem_node_ref[j : j + 1, LANES * h : LANES * (h + 1)])
             index_tables(row, nr, nc, 2 * j + h)
-    node_columns = columns_of(elem_node_ref[...])
+    node_columns = columns_of(padded(elem_node_ref[...]))
     for j in range(NDOF):
         for h in range(2):
             oh_n[256 * j + LANES * h : 256 * j + LANES * (h + 1), :] = one_hot(
@@ -432,24 +552,18 @@
             )
     masks(qm_n, nc, 2 * NDOF, NG)
 
+    finish_merge(M_IMAGE, [tot, tot2], link_e, inv_e, EB)
     sums = reduce_finish(1, 1)
     quotient = jnp.broadcast_to(sums[:, 0:1] / sums[:, 1:2], (8, LANES))
-    for k in range(EB):
+    for k in range(EG):
         residual = tot[k] - quotient * tot2[k]
         res[k] = residual
         first_step = residual * recip[k] * (1.0 / center)
         step[k] = first_step
         ve[k] = first_step
 
-    def stiff_image(extend, back):
-        gather([vv], er, ec, 2 * EDOF, [ve], 0, EB, 4)
-        arrived(extend)
-        for t in range(3):
-            tile = edge_tile(extend, 0, t, False)
-            if extend == X_FIRST:
-                tile = tile - quotient * edge_tile(extend, 1, t, False)
-            ve[EB + t] = tile
-        gather([vv], er, ec, 2 * EDOF, [ve], EB, EG, 4)
+    def stiff_terms():
+        gather([vv], er, ec, 2 * EDOF, [ve], 0, EG, 8)
 
         def consume(i, total, carry):
             keep_terms(0, None, 0, i, total)
@@ -457,105 +571,84 @@
 
         lax.fori_loop(0, 5, apply(stiff_ref, vv, EDOF, 4, consume), 0)
         product = scatter(48, ECOL, oh_e)
-        for t in range(3):
-            send_bufs[back][t, 0] = joined(product, t)
-            launch(back, t)
+        return [joined(product, t) for t in range(3)]
+
+    def stiff_owned():
         fill(0, qm_e, 0, EB, 2 * EDOF, 0)
         product = scatter(16 * EB, ECOL, oh_e)
         for k in range(EB):
             tot[k] = joined(product, k)
-        return back
-
-    def image_block(tiles, k):
-        return tot[k] + returned(inv_e, tiles, k, 2)
 
     sigma = center / spread
     rho_now = 1.0 / sigma
-    extend = X_FIRST
     for turn in range(CHEB_DEG - 1):
         rho_next = 1.0 / (2.0 * sigma - rho_now)
-        back = X_CHEB + 2 * turn
-        stiff_image(extend, back)
+        ghosts = stiff_terms()
+        far_start(M_CHEB + turn, [ghosts])
+        for t in range(3):
+            tot[EB + t] = ghosts[t]
+        stiff_owned()
+        near_start(
+            M_CHEB + turn,
+            [[pick(tot, sr, sc, t, EB) for t in range(3)]],
+            [[tot[EB + t] for t in range(3)]],
+        )
         if turn == 0:
+            loads[2].wait()
             for j in range(NDOF):
                 for h in range(2):
                     diagonal = spread_row(nodal_ref[j, j : j + 1, LANES * h : LANES * (h + 1)])
                     st[0:16, 256 * j + LANES * h : 256 * j + LANES * (h + 1)] = split(diagonal)
             fill(0, qm_n, 0, NG, 2 * NDOF, 0)
             product = scatter(16 * NG, NCOL, oh_n)
-            for t in range(3):
-                send_bufs[X_NDIAG][t, 0] = joined(product, NB + t // 2)
-                launch(X_NDIAG, t)
-            for k in range(NB):
+            for k in range(NG):
                 nrecip[k] = joined(product, k)
-            inverse_lists(inv_n, node_rows, tr, tc, 4, NB)
+            merge_start(M_NDIAG, [nrecip], tr, tc, NB)
         else:
             for side in range(2):
                 for k in range(EB):
-                    row = grad_ref[1 - side : 2 - side, LANES * k : LANES * (k + 1)]
+                    row = padded(grad_ref[1 - side : 2 - side, LANES * k : LANES * (k + 1)])
                     index_tables(row, gr, gc, side * EB + k)
-            grad_columns = columns_of(grad_ref[...])
+            grad_columns = columns_of(padded(grad_ref[...]))
             for side in range(2):
                 for k in range(EB):
                     oh_g[LANES * (side * EB + k) : LANES * (side * EB + k + 1), :] = one_hot(
                         grad_columns[LANES * k : LANES * (k + 1), 1 - side : 2 - side]
                     )
             masks(qm_g, gc, 2 * EB, NG)
-        arrived(back)
-        tiles = [edge_tile(back, 0, t, True) for t in range(3)]
-        for k in range(EB):
-            remain = res[k] - image_block(tiles, k)
+        finish_merge(M_CHEB + turn, [tot], link_e, inv_e, EB)
+        for k in range(EG):
+            remain = res[k] - tot[k]
             new_step = rho_next * rho_now * step[k] + (2.0 * rho_next / spread) * remain * recip[k]
             step[k] = new_step
             ve[k] = ve[k] + new_step
-        extend = back + 1
-        for t in range(3):
-            send_bufs[extend][t, 0] = pick(ve, sr, sc, t, EB)
-            launch(extend, t)
         rho_now = rho_next
-    back = X_CHEB + 4
-    stiff_image(extend, back)
-    arrived(X_NDIAG)
-    tiles = [node_tile(X_NDIAG, n, True) for n in range(2)]
-    for k in range(NB):
-        nrecip[k] = 1.0 / (nrecip[k] + returned(inv_n, tiles, k, 4))
-    arrived(back)
-    tiles = [edge_tile(back, 0, t, True) for t in range(3)]
+    ghosts = stiff_terms()
+    for t in range(3):
+        send_bufs[X_RETURN][t, 0] = ghosts[t]
+        launch(X_RETURN, t)
+    stiff_owned()
+    finish_merge(M_NDIAG, [nrecip], link_n, inv_n, NB)
+    for k in range(NG):
+        padding = jnp.logical_and(k >= NB, (lane8 & 63) >= 32)
+        nrecip[k] = 1.0 / jnp.where(padding, 1.0, nrecip[k])
+    arrived(X_RETURN)
+    tiles = [edge_tile(X_RETURN, 0, t, True) for t in range(3)]
     for k in range(EB):
-        after = split(res[k] - image_block(tiles, k))
+        after = split(res[k] - (tot[k] + returned(inv_e, tiles, k)))
         st[0:16, LANES * k : LANES * (k + 1)] = after
         st[0:16, LANES * (EB + k) : LANES * (EB + k + 1)] = -after
 
-    def node_return(e, qm, width, table, blocks):
-        fill(0, qm, NB, NG, blocks, 0)
-        product = scatter(32, width, table)
-        for t in range(3):
-            send_bufs[e][t, 0] = joined(product, t // 2)
-            launch(e, t)
-        fill(0, qm, 0, NB, blocks, 0)
-        product = scatter(48, width, table)
-        for k in range(NB):
+    def node_start(e, qm, width, table, blocks):
+        fill(0, qm, 0, NG, blocks, 0)
+        product = scatter(16 * NG, width, table)
+        for k in range(NG):
             ntot[k] = joined(product, k)
-
-    def node_sum(e):
-        arrived(e)
-        tiles = [node_tile(e, n, True) for n in range(2)]
-        return [ntot[k] + returned(inv_n, tiles, k, 4) for k in range(NB)]
-
-    def node_send(e):
-        picked = [pick(ne, tr, tc, n, NB) for n in range(2)]
-        for t in range(3):
-            send_bufs[e][t, 0] = picked[t // 2]
-            launch(e, t)
-
-    def node_ghosts(e):
-        arrived(e)
-        for n in range(2):
-            ne[NB + n] = node_tile(e, n, False)
-
-    node_return(X_NODE, qm_g, GCOL, oh_g, 2 * EB)
-
-    gather([vp], er, ec, 2 * EDOF, [pe], 0, EG, 4)
+        merge_start(e, [ntot], tr, tc, NB)
+
+    node_start(M_NODE, qm_g, GCOL, oh_g, 2 * EB)
+
+    gather([vp], er, ec, 2 * EDOF, [pe], 0, EG, 8)
 
     def p_consume(store):
         def consume(i, total, carry):
@@ -565,24 +658,21 @@
         return consume
 
     lax.fori_loop(0, 5, apply(stiff_ref, vp, EDOF, 4, p_consume(32)), 0)
-
-    for k, total in enumerate(node_sum(X_NODE)):
-        nres[k] = total
-        first = jacobi_weight * total * nrecip[k]
+    lax.fori_loop(0, 5, apply(mass_ref, vp, EDOF, 4, p_consume(48)), 0)
+    finish_merge(M_NODE, [ntot], link_n, inv_n, NB)
+    for k in range(NG):
+        nres[k] = ntot[k]
+        first = jacobi_weight * ntot[k] * nrecip[k]
         nfirst[k] = first
         ne[k] = first
-    node_send(X_NODE + 1)
-    gather([nv], nr, nc, 2 * NDOF, [ne], 0, NB, 4)
-    lax.fori_loop(0, 5, apply(mass_ref, vp, EDOF, 4, p_consume(48)), 0)
-    node_ghosts(X_NODE + 1)
-    gather([nv], nr, nc, 2 * NDOF, [ne], NB, NG, 4)
+    gather([nv], nr, nc, 2 * NDOF, [ne], 0, NG, 4)
 
     def node_consume(i, total, carry):
         st[pl.ds(0, 16), cols(i * LANES)] = split(total)
         return carry
 
     lax.fori_loop(0, 5, apply(nodal_ref, nv, NDOF, 2, node_consume), 0)
-    node_return(X_NODE + 2, qm_n, NCOL, oh_n, 2 * NDOF)
+    node_start(M_NODE + 1, qm_n, NCOL, oh_n, 2 * NDOF)
 
     def keep_basis(values, base):
         def body(i, carry):
@@ -593,12 +683,10 @@
 
     keep_basis(vx, 0)
     keep_basis(vp, 32)
-    for k, total in enumerate(node_sum(X_NODE + 2)):
-        ne[k] = nfirst[k] + jacobi_weight * (nres[k] - total) * nrecip[k]
-    node_send(X_NODE + 3)
-    gather([gv], gr, gc, 2 * EB, [ne], 0, NB, 4)
-    node_ghosts(X_NODE + 3)
-    gather([gv], gr, gc, 2 * EB, [ne], NB, NG, 4)
+    finish_merge(M_NODE + 1, [ntot], link_n, inv_n, NB)
+    for k in range(NG):
+        ne[k] = nfirst[k] + jacobi_weight * (nres[k] - ntot[k]) * nrecip[k]
+    gather([gv], gr, gc, 2 * EB, [ne], 0, NG, 4)
     for k in range(EB):
         total = ve[k] + gv[k] - gv[EB + k]
         ve[k] = total
@@ -648,8 +736,11 @@
         )
         out[...] = jnp.concatenate([upper, middle, lower], axis=0)
 
-    for e in range(len(COUNTS)):
+    for e in range(len(PLAIN)):
         whole(e).wait_send()
+    for e in range(len(MERGED)):
+        near_whole(e).wait_send()
+        far_whole(e).wait_send()
     for slot in range(4):
         reduce_whole(slot, slot % 2).wait_send()
 
@@ -668,6 +759,9 @@
             return pltpu.VMEM((rows, width), bf16)
 
         scratch = [
+            pltpu.VMEM(arrays[2].shape, f32),
+            pltpu.VMEM(arrays[3].shape, f32),
+            pltpu.VMEM(arrays[4].shape, f32),
             tiles(EG),
             tiles(EG),
             tiles(EG),
@@ -685,10 +779,12 @@
             integers(2 * EB),
             integers(3),
             integers(3),
-            integers(2),
-            integers(2),
+            integers(3),
+            integers(3),
             integers(6 * EB),
             integers(6 * NB),
+            integers(18),
+            integers(18),
             halves(ECOL, LANES),
             halves(16 * EG, ECOL),
             halves(NCOL, LANES),
@@ -699,21 +795,30 @@
             halves(32 * EB, ECOL),
             halves(48, ECOL),
             halves(128, ECOL),
-            tiles(EB),
-            tiles(EB),
-            tiles(EB),
-            tiles(EB),
-            tiles(EB),
-            tiles(NB),
-            tiles(NB),
-            tiles(NB),
-            tiles(NB),
-            [tiles(3, count) for count in COUNTS],
-            [tiles(6, count) for count in COUNTS],
+            tiles(EG),
+            tiles(EG),
+            tiles(EG),
+            tiles(EG),
+            tiles(EG),
+            tiles(NG),
+            tiles(NG),
+            tiles(NG),
+            tiles(NG),
+            [tiles(3, count) for count in PLAIN],
+            [tiles(6, count) for count in PLAIN],
+            [tiles(6, count) for count in MERGED],
+            [tiles(6, count) for count in MERGED],
+            [tiles(len(PAIRS), count) for count in MERGED],
+            [tiles(len(PAIRS), count) for count in MERGED],
             tiles(4),
             tiles(4, max(LOW, devices // LOW)),
-            pltpu.SemaphoreType.DMA((len(COUNTS),)),
-            pltpu.SemaphoreType.DMA((len(COUNTS),)),
+            pltpu.SemaphoreType.DMA((3,)),
+            pltpu.SemaphoreType.DMA((len(PLAIN),)),
+            pltpu.SemaphoreType.DMA((len(PLAIN),)),
+            pltpu.SemaphoreType.DMA((len(MERGED),)),
+            pltpu.SemaphoreType.DMA((len(MERGED),)),
+            pltpu.SemaphoreType.DMA((len(MERGED),)),
+            pltpu.SemaphoreType.DMA((len(MERGED),)),
             pltpu.SemaphoreType.DMA((4,)),
             pltpu.SemaphoreType.DMA((4,)),
         ]
@@ -725,7 +830,7 @@
                 jax.ShapeDtypeStruct((24, 24), f32),
                 jax.ShapeDtypeStruct((24, 24), f32),
             ),
-            in_specs=[vmem] * 10,
+            in_specs=[vmem] * 2 + [pl.BlockSpec(memory_space=pl.ANY)] * 3 + [vmem] * 5,
             out_specs=(vmem, vmem, vmem),
             scratch_shapes=scratch,
             compiler_params=pltpu.CompilerParams(

time: 115 us -> 97.6 us (0.85)
  Pallas kernels: 111 us -> 94 us
    pallas_call x1, Pallas kernels: 111 us -> 94 us  [shards(): pl.pallas_call(lambda *refs: kernel(devices, *refs), out_shape=(jax.Shape...]
where the time goes in v2:
time: 97.6 us; the launch traced here: 97.4 us
  Pallas kernels  94 us (96%)
  local copies, waits for them, and re-layouts  2.74 us (3%)
    pallas_call x1, Pallas kernels, shards(): pl.pallas_call(lambda *refs: kernel(devices, *refs), out_shape=(jax.Shape...  94 us
    unnamed x7, local copies, waits for them, and re-layouts  2.74 us

profile of v2, /device:TPU:1, one launch (start us, length us, event | category | flops | bytes accessed | tf_op | source)
XLA Modules:
  0.0 97.4 jit_solution(9143522661096650284)
XLA Ops:
  0.6 94.0 %shard_map.121 = (f32[8,1536]{1,0:T(8,128)}, f32[24,24]{1,0:T(8,128)}, f32[24,24]{1,0:T(8,128)}) custom-call(f32[8,1536]{1,0:T(8,128)} %refs_0_.1, f32[8,1536]{1,0:T(8,128)} %refs_1_.1, f32[20,20,256]{2,1,0:T(8,128)} %refs_2_.1, f32[20,20,256]{2,1,0:T(8,128)} %refs_3_.1, f32[10,10,256]{2,1,0:T(8,128)} %refs_4_.1, s32[20,256]{1,0:T(8,128)} %refs_5_.1, ...), custom_call_target="tpu_custom_call" | custom-call | tf_op jit(solution)/shard_map/pallas_call | solution.py:826
  94.6 0.0 copy-start.1
  94.6 1.4 %copy.16 = f32[8,1536]{1,0:T(8,128)} copy(f32[8,1536]{1,0:T(8,128)} %get-tuple-element.6) | data formatting | bytes 98304
  96.1 0.0 copy-done.1
  96.1 0.0 copy-start
  96.1 0.6 copy.17
  96.7 0.1 copy-done
  96.8 0.6 copy.18
Async XLA Ops:
  94.6 1.4 %copy-start.1 = (f32[24,24]{1,0:T(8,128)S(1)}, f32[24,24]{1,0:T(8,128)}, u32[]{:S(2)}) copy-start(f32[24,24]{1,0:T(8,128)} %get-tuple-element.7) | copy-start | bytes 6916
  96.1 0.7 copy-start

commit v3 on v2

--- a/solution.py
+++ b/solution.py
@@ -26,7 +26,10 @@
 bf16 = jnp.bfloat16
 MESH = pl.DeviceIdType.MESH
 
-PAIRS = [(a, b) for a in range(6) for b in range(a, 6) if b != a ^ 1]
+PAIRS = sorted(
+    [(a, b) for a in range(6) for b in range(a, 6) if b != a ^ 1],
+    key=lambda pair: [(1, 1), (1, 2), (2, 2), (0, 1), (0, 2), (0, 0)].index((pair[0] // 2, pair[1] // 2)),
+)
 X_PAIR, X_LINK, X_RETURN, X_W = 0, 1, 2, 3
 PLAIN = (2, 2, 1, 1)
 M_DIAG, M_IMAGE, M_CHEB, M_NDIAG, M_NODE = 0, 1, 2, 4, 5
@@ -350,7 +353,7 @@
                 qm[pl.ds(16 * q, 16), cols(i * LANES)] = jnp.concatenate([one, one], 0).astype(bf16)
             return carry
 
-        lax.fori_loop(0, count, body, 0, unroll=2)
+        lax.fori_loop(0, count, body, 0, unroll=4)
 
     def one_hot(column):
         return jnp.where(jnp.broadcast_to(column, (LANES, LANES)) == lane128, 1.0, 0.0).astype(bf16)
@@ -362,7 +365,7 @@
             rows = jnp.concatenate([rows, jnp.zeros((padded, width), jnp.int32)], axis=0)
         return (rows & 127).astype(f32).T
 
-    def fill(base, qm, first, last, count, source, unroll=2):
+    def fill(base, qm, first, last, count, source, unroll=10):
         def body(i, carry):
             term = st[pl.ds(source, 16), cols(i * LANES)]
             for q in range(first, last):
@@ -415,9 +418,6 @@
     for t in range(3):
         send_bufs[X_PAIR][t, 0] = pick(xe, sr, sc, t, EB)
         send_bufs[X_PAIR][t, 1] = pick(pe, sr, sc, t, EB)
-    pl.semaphore_wait(barrier, len(everyone))
-    for t in range(3):
-        launch(X_PAIR, t)
 
     for j in range(EDOF):
         for h in range(2):
@@ -447,9 +447,6 @@
         shares = [[pick(total, lanes, blocks, t, owned) for t in range(3)] for total in totals]
         near_start(e, shares, ghosts)
 
-    merge_start(M_DIAG, [recip], sr, sc, EB)
-
-    gather([vx], er, ec, 2 * EDOF, [xe], 0, EB, 4)
 
     def inverse_lists(inverse, rows, lanes, blocks, owned, i):
         turned = columns_of(jnp.concatenate(rows, axis=0))
@@ -477,14 +474,19 @@
     for t in range(3):
         index_tables(node_rows[t], tr, tc, t)
     inverse_lists(inv_n, node_rows, tr, tc, NB, 1)
+    pl.semaphore_wait(barrier, len(everyone))
+    for t in range(3):
+        launch(X_PAIR, t)
     for t in range(3):
         launch(X_LINK, t)
+    merge_start(M_DIAG, [recip], sr, sc, EB)
+    gather([vx], er, ec, 2 * EDOF, [xe], 0, EB, 20)
 
     arrived(X_PAIR)
     for t in range(3):
         xe[EB + t] = edge_tile(X_PAIR, 0, t, False)
         pe[EB + t] = edge_tile(X_PAIR, 1, t, False)
-    gather([vx], er, ec, 2 * EDOF, [xe], EB, EG, 4)
+    gather([vx], er, ec, 2 * EDOF, [xe], EB, EG, 20)
 
     def keep_terms(base, store, ghost_base, i, total):
         term = split(total)
@@ -504,8 +506,8 @@
         return consume
 
     loads[1].wait()
-    numerator = lax.fori_loop(0, 5, apply(stiff_ref, vx, EDOF, 4, x_consume(0, 0, 0)), zero8)
-    denominator = lax.fori_loop(0, 5, apply(mass_ref, vx, EDOF, 4, x_consume(16, 16, 48)), zero8)
+    numerator = lax.fori_loop(0, 5, apply(stiff_ref, vx, EDOF, 4, x_consume(0, 0, 0)), zero8, unroll=5)
+    denominator = lax.fori_loop(0, 5, apply(mass_ref, vx, EDOF, 4, x_consume(16, 16, 48)), zero8, unroll=5)
     numerator = jnp.sum(numerator, axis=1, keepdims=True)
     denominator = jnp.sum(denominator, axis=1, keepdims=True)
     reduce_start(0, 0, jnp.where(lane8 == 0, numerator, jnp.where(lane8 == 1, denominator, 0.0)))
@@ -553,8 +555,19 @@
     masks(qm_n, nc, 2 * NDOF, NG)
 
     finish_merge(M_IMAGE, [tot, tot2], link_e, inv_e, EB)
+    for k in range(EG):
+        scaled = recip[k] * (1.0 / center)
+        ve[k] = tot[k] * scaled
+        step[k] = tot2[k] * scaled
+    gather([vv, vp], er, ec, 2 * EDOF, [ve, step], 0, EG, 20)
     sums = reduce_finish(1, 1)
     quotient = jnp.broadcast_to(sums[:, 0:1] / sums[:, 1:2], (8, LANES))
+
+    def combine(i, carry):
+        vv[i] = vv[i] - quotient * vp[i]
+        return carry
+
+    lax.fori_loop(0, 2 * EDOF, combine, 0, unroll=8)
     for k in range(EG):
         residual = tot[k] - quotient * tot2[k]
         res[k] = residual
@@ -562,14 +575,15 @@
         step[k] = first_step
         ve[k] = first_step
 
-    def stiff_terms():
-        gather([vv], er, ec, 2 * EDOF, [ve], 0, EG, 8)
+    def stiff_terms(gathered):
+        if not gathered:
+            gather([vv], er, ec, 2 * EDOF, [ve], 0, EG, 20)
 
         def consume(i, total, carry):
             keep_terms(0, None, 0, i, total)
             return carry
 
-        lax.fori_loop(0, 5, apply(stiff_ref, vv, EDOF, 4, consume), 0)
+        lax.fori_loop(0, 5, apply(stiff_ref, vv, EDOF, 4, consume), 0, unroll=5)
         product = scatter(48, ECOL, oh_e)
         return [joined(product, t) for t in range(3)]
 
@@ -583,7 +597,7 @@
     rho_now = 1.0 / sigma
     for turn in range(CHEB_DEG - 1):
         rho_next = 1.0 / (2.0 * sigma - rho_now)
-        ghosts = stiff_terms()
+        ghosts = stiff_terms(turn == 0)
         far_start(M_CHEB + turn, [ghosts])
         for t in range(3):
             tot[EB + t] = ghosts[t]
@@ -623,7 +637,7 @@
             step[k] = new_step
             ve[k] = ve[k] + new_step
         rho_now = rho_next
-    ghosts = stiff_terms()
+    ghosts = stiff_terms(False)
     for t in range(3):
         send_bufs[X_RETURN][t, 0] = ghosts[t]
         launch(X_RETURN, t)
@@ -648,7 +662,7 @@
 
     node_start(M_NODE, qm_g, GCOL, oh_g, 2 * EB)
 
-    gather([vp], er, ec, 2 * EDOF, [pe], 0, EG, 8)
+    gather([vp], er, ec, 2 * EDOF, [pe], 0, EG, 20)
 
     def p_consume(store):
         def consume(i, total, carry):
@@ -657,21 +671,21 @@
 
         return consume
 
-    lax.fori_loop(0, 5, apply(stiff_ref, vp, EDOF, 4, p_consume(32)), 0)
-    lax.fori_loop(0, 5, apply(mass_ref, vp, EDOF, 4, p_consume(48)), 0)
+    lax.fori_loop(0, 5, apply(stiff_ref, vp, EDOF, 4, p_consume(32)), 0, unroll=5)
+    lax.fori_loop(0, 5, apply(mass_ref, vp, EDOF, 4, p_consume(48)), 0, unroll=5)
     finish_merge(M_NODE, [ntot], link_n, inv_n, NB)
     for k in range(NG):
         nres[k] = ntot[k]
         first = jacobi_weight * ntot[k] * nrecip[k]
         nfirst[k] = first
         ne[k] = first
-    gather([nv], nr, nc, 2 * NDOF, [ne], 0, NG, 4)
+    gather([nv], nr, nc, 2 * NDOF, [ne], 0, NG, 20)
 
     def node_consume(i, total, carry):
         st[pl.ds(0, 16), cols(i * LANES)] = split(total)
         return carry
 
-    lax.fori_loop(0, 5, apply(nodal_ref, nv, NDOF, 2, node_consume), 0)
+    lax.fori_loop(0, 5, apply(nodal_ref, nv, NDOF, 2, node_consume), 0, unroll=5)
     node_start(M_NODE + 1, qm_n, NCOL, oh_n, 2 * NDOF)
 
     def keep_basis(values, base):
@@ -679,14 +693,14 @@
             basis_t[pl.ds(base, 16), cols(i * LANES)] = split(values[i])
             return carry
 
-        lax.fori_loop(0, 2 * EDOF, body, 0, unroll=4)
+        lax.fori_loop(0, 2 * EDOF, body, 0, unroll=10)
 
     keep_basis(vx, 0)
     keep_basis(vp, 32)
     finish_merge(M_NODE + 1, [ntot], link_n, inv_n, NB)
     for k in range(NG):
         ne[k] = nfirst[k] + jacobi_weight * (nres[k] - ntot[k]) * nrecip[k]
-    gather([gv], gr, gc, 2 * EB, [ne], 0, NG, 4)
+    gather([gv], gr, gc, 2 * EB, [ne], 0, NG, 24)
     for k in range(EB):
         total = ve[k] + gv[k] - gv[EB + k]
         ve[k] = total
@@ -696,13 +710,13 @@
         send_bufs[X_W][t, 0] = pick(ve, sr, sc, t, EB)
         launch(X_W, t)
     image_t[96:128, :] = jnp.zeros((32, ECOL), bf16)
-    gather([vv], er, ec, 2 * EDOF, [ve], 0, EB, 4)
+    gather([vv], er, ec, 2 * EDOF, [ve], 0, EB, 20)
     arrived(X_W)
     for t in range(3):
         ve[EB + t] = edge_tile(X_W, 0, t, False)
-    gather([vv], er, ec, 2 * EDOF, [ve], EB, EG, 4)
-    lax.fori_loop(0, 5, apply(stiff_ref, vv, EDOF, 4, p_consume(64)), 0)
-    lax.fori_loop(0, 5, apply(mass_ref, vv, EDOF, 4, p_consume(80)), 0)
+    gather([vv], er, ec, 2 * EDOF, [ve], EB, EG, 20)
+    lax.fori_loop(0, 5, apply(stiff_ref, vv, EDOF, 4, p_consume(64)), 0, unroll=5)
+    lax.fori_loop(0, 5, apply(mass_ref, vv, EDOF, 4, p_consume(80)), 0, unroll=5)
     keep_basis(vv, 16)
     product = lax.dot_general(
         basis_t[...], image_t[...], (((1,), (1,)), ((), ())), preferred_element_type=f32

time: 97.6 us -> 94 us (0.963)
  Pallas kernels: 94 us -> 90.3 us
    pallas_call x1, Pallas kernels: 94 us -> 90.3 us  [shards(): pl.pallas_call(lambda *refs: kernel(devices, *refs), out_shape=(jax.Shape...]
where the time goes in v3:
time: 94 us; the launch traced here: 93.7 us
  Pallas kernels  90.3 us (96%)
  local copies, waits for them, and re-layouts  2.74 us (3%)
    pallas_call x1, Pallas kernels, shards(): pl.pallas_call(lambda *refs: kernel(devices, *refs), out_shape=(jax.Shape...  90.3 us
    unnamed x7, local copies, waits for them, and re-layouts  2.74 us

profile of v3, /device:TPU:1, one launch (start us, length us, event | category | flops | bytes accessed | tf_op | source)
XLA Modules:
  0.0 93.7 jit_solution(598342873887939202)
XLA Ops:
  0.6 90.3 %shard_map.121 = (f32[8,1536]{1,0:T(8,128)}, f32[24,24]{1,0:T(8,128)}, f32[24,24]{1,0:T(8,128)}) custom-call(f32[8,1536]{1,0:T(8,128)} %refs_0_.1, f32[8,1536]{1,0:T(8,128)} %refs_1_.1, f32[20,20,256]{2,1,0:T(8,128)} %refs_2_.1, f32[20,20,256]{2,1,0:T(8,128)} %refs_3_.1, f32[10,10,256]{2,1,0:T(8,128)} %refs_4_.1, s32[20,256]{1,0:T(8,128)} %refs_5_.1, ...), custom_call_target="tpu_custom_call" | custom-call | tf_op jit(solution)/shard_map/pallas_call | solution.py:840
  91.0 0.0 copy-start.1
  91.0 1.4 %copy.16 = f32[8,1536]{1,0:T(8,128)} copy(f32[8,1536]{1,0:T(8,128)} %get-tuple-element.6) | data formatting | bytes 98304
  92.4 0.0 copy-done.1
  92.4 0.0 copy-start
  92.4 0.6 copy.17
  93.0 0.1 copy-done
  93.1 0.6 copy.18
Async XLA Ops:
  91.0 1.4 %copy-start.1 = (f32[24,24]{1,0:T(8,128)S(1)}, f32[24,24]{1,0:T(8,128)}, u32[]{:S(2)}) copy-start(f32[24,24]{1,0:T(8,128)} %get-tuple-element.7) | copy-start | bytes 6916
  92.4 0.7 copy-start
